TPU v7x, 128 devices: a whole 4x4x4 slice. The times are simulated.
128 devices in a mesh: seq: 16 (over x, y), grp: 8 (over z, core).
Axes of the slice: x: 4, y: 4, z: 4, core: 2. Of those that a mesh axis runs over, the one named last changes fastest.
Arguments:
- queries: bfloat16 [8, 16, 128, 2560], P('grp', 'seq'), may hold values from -140 to 140
- out_grad: bfloat16 [8, 16, 128, 2560], P('grp', 'seq'), may hold values from -48 to 48
- saved_output: bfloat16 [8, 16, 128, 2560], P('grp', 'seq'), may hold values from -3 to 3
- key_rows: bfloat16 [8, 16, 128, 512], P('grp', 'seq'), may hold values from -6 to 6
- value_rows: bfloat16 [8, 16, 128, 512], P('grp', 'seq'), may hold values from -6 to 6
- hidden_rows: bfloat16 [8, 16, 128, 5120], P('grp', 'seq'), may hold values from -6 to 6
- prefix_keys: bfloat16 [8, 128, 512], replicated, may hold values from -8 to 8
- prefix_values: bfloat16 [8, 128, 512], replicated, may hold values from -6 to 6
- prefix_hidden: bfloat16 [8, 128, 5120], P('grp', 'seq'), may hold values from -6 to 6
- block_mask: int32 [8, 16, 16], P('grp'), may hold values from 0 to 1, as said below
- prefix_list: int32 [8, 2], P('grp'), may hold values from 0 to 7, as said below
- key_down: bfloat16 [5120, 64], replicated, may hold values from -0.078125 to 0.078125
- value_down: bfloat16 [5120, 64], replicated, may hold values from -0.078125 to 0.078125
- key_up: bfloat16 [64, 512], replicated, may hold values from -0.75 to 0.75
- value_up: bfloat16 [64, 512], replicated, may hold values from -0.75 to 0.75
Outputs:
- pair_grads: bfloat16 [8, 2048, 1024], P('grp', 'seq')
- prefix_grads: float32 [8, 128, 1024], P('grp', 'seq')
- down_grads: float32 [2, 5120, 64], replicated
- up_grads: float32 [2, 64, 512], replicated
Inputs may be any that keep to these rules, and one draw needn't show every extreme that they name: block_mask[g, i, j] is 1 where j = i and 0 where j > i. `prefix_list`: each row names 2 distinct prefix blocks.
All inputs are finite; a program needn't handle non-finite values.
Results may differ from a plain program's by a relative error of at most 0.024.
Values may be sent and summed in bfloat16 or wider, within the bound.
A program may use at most 128 MiB of HBM per device.

v0:
```python
import jax
import jax.numpy as jnp
from jax import lax
from jax.sharding import PartitionSpec as P

HEAD_SIZE = 128
RANK = 64
BLK = 128


adapter_scale = 2.0
masked_score = -1e30


def visible_table(mask_rows, slice_index, token_count, sequence_total):
    span = token_count // sequence_total
    local = jnp.arange(token_count, dtype=jnp.int32)
    query_place = local // span * token_count + slice_index * span + local % span
    key_index = jnp.arange(sequence_total * token_count, dtype=jnp.int32)
    key_rest = key_index % token_count
    key_place = key_rest // span * token_count + key_index // token_count * span + key_rest % span
    picked = jnp.take(mask_rows, query_place // BLK, axis=0)
    broadcast_copies = jnp.take(picked, key_place // BLK, axis=1)
    same_block = query_place[:, None] // BLK == key_place[None, :] // BLK
    causal = key_place[None, :] <= query_place[:, None]
    return (broadcast_copies == 1) & (jnp.logical_not(same_block) | causal)


def head_grads(query_head, grad_head, key_head, value_head, allowed, log_total, delta_head):
    scale_factor = HEAD_SIZE ** (-0.5)
    scores = (
        jnp.einsum("tgd,kd->tgk", query_head, key_head, preferred_element_type=jnp.float32)
        * scale_factor
    )
    attention = jnp.exp(scores - log_total[:, :, None])
    if allowed is not None:
        attention = jnp.where(allowed[:, None, :], attention, 0.0)
    attention_low = attention.astype(jnp.bfloat16)
    grad_attention = jnp.einsum(
        "tgd,kd->tgk", grad_head, value_head, preferred_element_type=jnp.float32
    )
    grad_scores = (attention * (grad_attention - delta_head[:, :, None]) * scale_factor).astype(
        jnp.bfloat16
    )
    key_grad = jnp.einsum(
        "tgk,tgd->kd", grad_scores, query_head, preferred_element_type=jnp.float32
    )
    value_grad = jnp.einsum(
        "tgk,tgd->kd", attention_low, grad_head, preferred_element_type=jnp.float32
    )
    return (key_grad, value_grad)


def inner_rows(former, latter):
    return lax.dot_general(
        former, latter, (((0,), (0,)), ((), ())), preferred_element_type=jnp.float32
    )


def on_device(
    queries,
    out_grad,
    saved_output,
    key_rows,
    value_rows,
    hidden_rows,
    prefix_keys,
    prefix_values,
    prefix_hidden,
    block_mask,
    prefix_list,
    key_down,
    value_down,
    key_up,
    value_up,
):
    sequence_total = lax.axis_size("seq")
    group_total = lax.axis_size("grp")
    slice_index = lax.axis_index("seq")
    token_count = queries.shape[2]
    slice_span = token_count // sequence_total
    pairing_width = key_rows.shape[3]
    heads_kv = pairing_width // HEAD_SIZE
    rollouts_per_group = queries.shape[3] // pairing_width
    scale_factor = HEAD_SIZE ** (-0.5)

    def by_slice(source):
        return source[0, 0].reshape(sequence_total, slice_span, source.shape[3])

    pair_local = jnp.concatenate([key_rows[0, 0], value_rows[0, 0]], axis=-1).reshape(
        sequence_total, slice_span, 2 * pairing_width
    )
    arrived = (
        lax.all_to_all(by_slice(queries), "seq", split_axis=0, concat_axis=0, tiled=True),
        lax.all_to_all(by_slice(out_grad), "seq", split_axis=0, concat_axis=0, tiled=True),
        lax.all_to_all(by_slice(saved_output), "seq", split_axis=0, concat_axis=0, tiled=True),
        lax.all_to_all(pair_local, "seq", split_axis=0, concat_axis=0, tiled=True),
        lax.all_to_all(by_slice(hidden_rows), "seq", split_axis=0, concat_axis=0, tiled=True),
    )
    hidden_tree = arrived[4].reshape(token_count, -1)
    query_tree = arrived[0].reshape(token_count, -1)
    grad_tree = arrived[1].reshape(token_count, -1)
    saved_tree = arrived[2].reshape(token_count, -1)
    pair_tree = arrived[3].reshape(token_count, -1)
    tree_pairs = lax.all_gather(pair_tree, "seq", axis=0, tiled=True)
    listed = prefix_list[0]
    listed_count = listed.shape[0]
    prefix_pairs = jnp.concatenate(
        [jnp.take(prefix_keys, listed, axis=0), jnp.take(prefix_values, listed, axis=0)], axis=-1
    ).reshape(listed_count * BLK, 2 * pairing_width)
    allowed = visible_table(block_mask[0], slice_index, token_count, sequence_total)
    delta_row_values = jnp.sum(
        (grad_tree.astype(jnp.float32) * saved_tree.astype(jnp.float32)).reshape(
            token_count, heads_kv, rollouts_per_group, HEAD_SIZE
        ),
        axis=-1,
    )
    query_heads, grad_heads, log_totals = ([], [], [])
    prefix_key_parts, prefix_value_parts = ([], [])
    for head_position in range(heads_kv):
        offset = head_position * rollouts_per_group * HEAD_SIZE
        query_head = query_tree[:, offset : offset + rollouts_per_group * HEAD_SIZE].reshape(
            token_count, rollouts_per_group, HEAD_SIZE
        )
        grad_head = grad_tree[:, offset : offset + rollouts_per_group * HEAD_SIZE].reshape(
            token_count, rollouts_per_group, HEAD_SIZE
        )
        key_head = tree_pairs[:, head_position * HEAD_SIZE : (head_position + 1) * HEAD_SIZE]
        prefix_key = prefix_pairs[:, head_position * HEAD_SIZE : (head_position + 1) * HEAD_SIZE]
        prefix_value = prefix_pairs[
            :,
            pairing_width
            + head_position * HEAD_SIZE : pairing_width
            + (head_position + 1) * HEAD_SIZE,
        ]
        scores = jnp.where(
            allowed[:, None, :],
            jnp.einsum("tgd,kd->tgk", query_head, key_head, preferred_element_type=jnp.float32)
            * scale_factor,
            masked_score,
        )
        prefix_scores = (
            jnp.einsum("tgd,kd->tgk", query_head, prefix_key, preferred_element_type=jnp.float32)
            * scale_factor
        )
        largest = jnp.maximum(jnp.max(scores, axis=-1), jnp.max(prefix_scores, axis=-1))
        summed = jnp.sum(jnp.exp(scores - largest[:, :, None]), axis=-1) + jnp.sum(
            jnp.exp(prefix_scores - largest[:, :, None]), axis=-1
        )
        log_total = largest + jnp.log(summed)
        prefix_key_grad, prefix_value_grad = head_grads(
            query_head,
            grad_head,
            prefix_key,
            prefix_value,
            None,
            log_total,
            delta_row_values[:, head_position],
        )
        query_heads.append(query_head)
        grad_heads.append(grad_head)
        log_totals.append(log_total)
        prefix_key_parts.append(prefix_key_grad)
        prefix_value_parts.append(prefix_value_grad)
    prefix_term = jnp.concatenate(prefix_key_parts + prefix_value_parts, axis=-1)
    key_parts = []
    value_parts = []
    for head_position in range(heads_kv):
        key_head = tree_pairs[:, head_position * HEAD_SIZE : (head_position + 1) * HEAD_SIZE]
        value_head = tree_pairs[
            :,
            pairing_width
            + head_position * HEAD_SIZE : pairing_width
            + (head_position + 1) * HEAD_SIZE,
        ]
        key_grad, value_grad = head_grads(
            query_heads[head_position],
            grad_heads[head_position],
            key_head,
            value_head,
            allowed,
            log_totals[head_position],
            delta_row_values[:, head_position],
        )
        key_parts.append(key_grad)
        value_parts.append(value_grad)
    pair_sum = lax.psum_scatter(
        jnp.concatenate(key_parts + value_parts, axis=-1).astype(jnp.bfloat16),
        "seq",
        scatter_dimension=0,
        tiled=True,
    )
    pool_count = prefix_keys.shape[0]
    owned_blocks = pool_count // group_total
    block_share = BLK // sequence_total
    chooser = (jnp.arange(pool_count, dtype=jnp.int32)[:, None] == listed[None, :]).astype(
        jnp.float32
    )
    dense_pool = jnp.dot(
        chooser, prefix_term.reshape(listed_count, -1), precision=lax.Precision.HIGHEST
    )
    dense_pool = dense_pool.reshape(
        group_total, owned_blocks, sequence_total, block_share, 2 * pairing_width
    )
    dense_pool = jnp.transpose(dense_pool, (2, 0, 1, 3, 4)).reshape(
        sequence_total * group_total * owned_blocks, block_share, 2 * pairing_width
    )
    prefix_grads = lax.psum_scatter(dense_pool, ("seq", "grp"), scatter_dimension=0, tiled=True)
    all_hidden = jnp.concatenate(
        [hidden_tree, prefix_hidden.reshape(-1, prefix_hidden.shape[2])], axis=0
    )
    all_grads = jnp.concatenate(
        [pair_sum, prefix_grads.astype(jnp.bfloat16).reshape(-1, 2 * pairing_width)], axis=0
    )
    down_pair = jnp.concatenate([key_down, value_down], axis=1)
    projected = jnp.dot(all_hidden, down_pair, preferred_element_type=jnp.float32).astype(
        jnp.bfloat16
    )
    contract_last = (((1,), (1,)), ((), ()))
    back_key = lax.dot_general(
        all_grads[:, :pairing_width], key_up, contract_last, preferred_element_type=jnp.float32
    )
    back_value = lax.dot_general(
        all_grads[:, pairing_width:], value_up, contract_last, preferred_element_type=jnp.float32
    )
    back_rows = jnp.concatenate([back_key, back_value], axis=1).astype(jnp.bfloat16)
    down_all = inner_rows(all_hidden, back_rows)
    multiplier = adapter_scale / (group_total * sequence_total)
    down_terms = jnp.stack([down_all[:, :RANK], down_all[:, RANK:]]) * multiplier
    up_key = inner_rows(projected[:, :RANK], all_grads[:, :pairing_width])
    up_value = inner_rows(projected[:, RANK:], all_grads[:, pairing_width:])
    up_terms = jnp.stack([up_key, up_value]) * multiplier
    down_grads, up_grads = lax.psum((down_terms, up_terms), ("seq", "grp"))
    return (pair_sum[None], prefix_grads, down_grads, up_grads)


def solution(mesh):
    in_specs = (
        P("grp", "seq", None, None),
        P("grp", "seq", None, None),
        P("grp", "seq", None, None),
        P("grp", "seq", None, None),
        P("grp", "seq", None, None),
        P("grp", "seq", None, None),
        P(),
        P(),
        P("grp", "seq", None),
        P("grp", None, None),
        P("grp", None),
        P(),
        P(),
        P(),
        P(),
    )
    out_specs = (P("grp", "seq", None), P("grp", "seq", None), P(), P())
    return jax.shard_map(
        on_device, mesh=mesh, in_specs=in_specs, out_specs=out_specs, check_vma=False
    )
```

profile of v0, /device:TPU:1, one launch (start us, length us, event | category | flops | bytes accessed | tf_op | source)
XLA Modules:
  0.0 1021.3 jit_solution(2774420747607639024)
XLA Ops:
  8.3 14.9 %all_to_all.25 = bf16[16,8,1024]{2,1,0:T(8,128)(2,1)} all-to-all(bf16[16,8,1024]{2,1,0:T(8,128)(2,1)S(1)} %pad_maximum_fusion.5), channel_id=1, replica_groups=mesh['seq'=16,'grp'=8] {'seq'}, dimensions={0} | all-to-all | bytes 524288 | tf_op jit(solution)/shard_map/all_to_all | solution.py:97
  23.3 3.6 all-to-all-start.1
  32.3 4.3 all-to-all-done.1
  36.6 4.2 all-to-all-start.2
  40.9 5.5 gather_fusion.1
  48.2 3.4 all-to-all-done.2
  51.6 3.9 all-to-all-start.3
  60.4 6.3 all-to-all-done.3
  79.2 5.4 all-gather.2.cloned.1.call-done
  86.4 3.5 fusion.19
  90.0 2.4 fusion.131
  92.5 5.2 exponential_reduce_fusion
  97.8 2.7 exponential_reduce_fusion.1
  100.8 2.1 fusion.109
  102.9 2.1 fusion.111
  107.0 2.1 fusion.115
  118.9 2.6 convolution_bitcast_fusion.4
  121.5 5.2 copy.270
  127.1 5.8 fusion.49
  132.9 5.8 fusion.51
  138.7 5.8 fusion.53
  144.6 5.7 fusion.55
  150.3 4.7 fusion.68
  155.0 4.7 fusion.71
  159.7 2.1 fusion.74
  161.8 2.3 fusion.77
  164.1 6.4 copy.306
  170.6 19.4 %all_to_all.26 = bf16[16,8,5120]{2,1,0:T(8,128)(2,1)S(1)} all-to-all(bf16[16,8,5120]{2,1,0:T(8,128)(2,1)} %bitcast.460), channel_id=1, replica_groups=mesh['seq'=16,'grp'=8] {'seq'}, dimensions={0} | all-to-all | bytes 2621440 | tf_op jit(solution)/shard_map/all_to_all | solution.py:98
  191.6 579.8 %reduce-scatter.5.cloned.1.call-done = f32[1,8,1024]{2,1,0:T(8,128)} async-done(((f32[128,8,1024]{2,1,0:T(8,128)}), f32[1,8,1024]{2,1,0:T(8,128)}) %reduce-scatter.5.cloned.1.call-update) | async-done | bytes 32784 | tf_op jit(solution)/shard_map/reduce_scatter | solution.py:208
  772.4 79.1 %reduce-scatter.7.cloned.1.call-done = bf16[128,1024]{1,0:T(8,128)(2,1)} async-done(((bf16[2048,1024]{1,0:T(8,128)(2,1)}), bf16[128,1024]{1,0:T(8,128)(2,1)}) %reduce-scatter.7.cloned.1.call-update) | async-done | bytes 262160
  857.5 152.8 %all-reduce.3.cloned.1.call-done = (f32[2,5120,64]{1,2,0:T(8,128)}, f32[2,64,512]{2,1,0:T(8,128)}) async-done(((f32[2,5120,64]{1,2,0:T(8,128)}, f32[2,64,512]{2,1,0:T(8,128)}), (f32[2,5120,64]{1,2,0:T(8,128)}, f32[2,64,512]{2,1,0:T(8,128)})) %all-reduce.3.cloned.1.call-update) | async-done | bytes 2883600 | tf_op jit(solution)/shard_map/psum | solution.py:233
  1010.3 3.5 copy.324
  (143 shorter events, 49.4 us)
Async XLA Ops:
  7.2 21.2 %copy-start = (bf16[8,128,512]{2,1,0:T(8,128)(2,1)S(1)}, bf16[8,128,512]{2,1,0:T(8,128)(2,1)}, u32[]{:S(2)}) copy-start(bf16[8,128,512]{2,1,0:T(8,128)(2,1)} %param.23) | copy-start | bytes 3145732
  7.2 77.4 %all-gather.2.cloned.1.call-start = ((), (), s32[]{:S(2)}) async-start(), calls=%async_computation.7 | async-start | bytes 4456448 | tf_op jit(solution)/shard_map/all_gather | solution.py:105
  23.3 13.3 %all-to-all-start.1 = ((bf16[16,8,2560]{2,1,0:T(8,128)(2,1)}), bf16[16,8,2560]{2,1,0:T(8,128)(2,1)S(1)}, u32[]{:S(2)}, u32[]{:S(2)}) async-start(bf16[16,8,2560]{2,1,0:T(8,128)(2,1)} %bitcast.474), calls=%async_computation.1 | async-start | bytes 1310720 | tf_op jit(solution)/shard_map/all_to_all | solution.py:94
  36.6 15.0 %all-to-all-start.2 = ((bf16[16,8,2560]{2,1,0:T(8,128)(2,1)}), bf16[16,8,2560]{2,1,0:T(8,128)(2,1)S(1)}, u32[]{:S(2)}, u32[]{:S(2)}) async-start(bf16[16,8,2560]{2,1,0:T(8,128)(2,1)} %bitcast.475), calls=%async_computation.2 | async-start | bytes 1310720 | tf_op jit(solution)/shard_map/all_to_all | solution.py:95
  51.6 15.1 %all-to-all-start.3 = ((bf16[16,8,2560]{2,1,0:T(8,128)(2,1)}), bf16[16,8,2560]{2,1,0:T(8,128)(2,1)S(1)}, u32[]{:S(2)}, u32[]{:S(2)}) async-start(bf16[16,8,2560]{2,1,0:T(8,128)(2,1)} %bitcast.476), calls=%async_computation.3 | async-start | bytes 1310720 | tf_op jit(solution)/shard_map/all_to_all | solution.py:96
  55.5 715.9 %reduce-scatter.5.cloned.1.call-start = ((), (), s32[]{:S(2)}) async-start(), calls=%async_computation.8 | async-start | bytes 4227072 | tf_op jit(solution)/shard_map/reduce_scatter | solution.py:208
  57.0 43.8 %copy-start.8 = (bf16[128,640]{0,1:T(8,128)(2,1)}, bf16[128,640]{0,1:T(8,128)(2,1)S(1)}, u32[]{:S(2)}) copy-start(bf16[128,640]{0,1:T(8,128)(2,1)S(1)} %copy.221) | copy-start | bytes 491524
  58.0 47.0 %copy-start.6 = (bf16[128,640]{0,1:T(8,128)(2,1)}, bf16[128,640]{0,1:T(8,128)(2,1)S(1)}, u32[]{:S(2)}) copy-start(bf16[128,640]{0,1:T(8,128)(2,1)S(1)} %copy.235) | copy-start | bytes 491524
  67.9 4.9 copy-start.14
  67.9 5.7 copy-start.13
  86.4 6.0 copy-start.2
  89.9 7.7 copy-start.4
  92.4 5.3 copy-start.3
  105.0 14.0 %copy-start.22 = (s32[1,2]{1,0:T(1,128)S(1)}, s32[1,2]{1,0:T(1,128)}, u32[]{:S(2)}) copy-start(s32[1,2]{1,0:T(1,128)} %param.27) | copy-start | bytes 28
  121.5 5.5 copy-start.9
  121.5 5.5 copy-start.15
  126.8 6.1 copy-start.12
  126.8 6.1 copy-start.18
  126.8 724.7 %reduce-scatter.7.cloned.1.call-start = ((), (), s32[]{:S(2)}) async-start(), calls=%async_computation.9 | async-start | bytes 4456448
  132.9 5.8 copy-start.7
  132.9 5.8 copy-start.17
  138.7 5.9 copy-start.10
  138.7 5.9 copy-start.16
  150.3 9.4 slice-start
  155.0 4.7 slice-start.1
  155.0 6.7 slice-start.2
  170.5 19.5 %copy-start.20 = (bf16[1,8,5120]{2,1,0:T(8,128)(2,1)S(1)}, bf16[1,8,5120]{2,1,0:T(8,128)(2,1)}, u32[]{:S(2)}) copy-start(bf16[1,8,5120]{2,1,0:T(8,128)(2,1)} %param.25) | copy-start | bytes 245764
  170.5 19.5 %copy-start.23 = (bf16[5120,64]{0,1:T(8,128)(2,1)S(1)}, bf16[5120,64]{0,1:T(8,128)(2,1)}, u32[]{:S(2)}) copy-start(bf16[5120,64]{0,1:T(8,128)(2,1)} %param.29) | copy-start | bytes 1966084
  170.5 682.6 %copy-start.24 = (bf16[64,512]{1,0:T(8,128)(2,1)S(1)}, bf16[64,512]{1,0:T(8,128)(2,1)}, u32[]{:S(2)}) copy-start(bf16[64,512]{1,0:T(8,128)(2,1)} %param.30) | copy-start | bytes 196612
  170.5 682.8 %copy-start.21 = (bf16[64,512]{1,0:T(8,128)(2,1)S(1)}, bf16[64,512]{1,0:T(8,128)(2,1)}, u32[]{:S(2)}) copy-start(bf16[64,512]{1,0:T(8,128)(2,1)} %param.31) | copy-start | bytes 196612
  170.5 839.8 %all-reduce.3.cloned.1.call-start = ((), (), s32[]{:S(2)}) async-start(), calls=%async_computation.10 | async-start | bytes 5767168 | tf_op jit(solution)/shard_map/psum | solution.py:233
  854.9 159.6 %copy-start.1 = (bf16[8,128,512]{2,1,0:T(8,128)(2,1)S(1)}, bf16[8,128,512]{2,1,0:T(8,128)(2,1)}, u32[]{:S(2)}) copy-start(bf16[8,128,512]{2,1,0:T(8,128)(2,1)} %param.23) | copy-start | bytes 3145732
  (4 other events, 11.0 us)
Sparse Core Ops, SparseCore 0:
  23.4 61.1 all-gather.1
  126.9 644.4 reduce-scatter.4
  775.1 76.3 reduce-scatter.6
  856.9 153.3 all-reduce.2
where the time goes:
time: 1030 us; the launch traced here: 1020 us
  waiting for transfers between devices  831 us (81%)
  matrix products  75.6 us (7%)
  local copies, waits for them, and re-layouts  39.4 us (4%)
  blocking collectives  34.3 us (3%)
  between operations  14.6 us (1%)
  other arithmetic  13.9 us (1%)
  starting transfers between devices  12.4 us (1%)
    reduce_scatter x1, waiting for transfers between devices, on_device(): lax.psum_scatter(dense_pool, ('seq', 'grp'), scatter_dimension=0, tiled=T...  580 us
    psum x1, waiting for transfers between devices, on_device(): down_grads, up_grads = lax.psum((down_terms, up_terms), ('seq', 'grp'))  153 us
    unnamed x5, waiting for transfers between devices  79.2 us
    dot_general x8, matrix products, head_grads(): jnp.einsum('tgk,tgd->kd', grad_scores, query_head, preferred_element_type...  31.6 us
    dot_general x8, matrix products, head_grads(): jnp.einsum('tgk,tgd->kd', attention_low, grad_head, preferred_element_typ...  21.1 us
  transfers between devices with their start and end apart: 7, of which 7 were waited for; matrix products, arithmetic and copies ran while one was open for 7% of the time, Pallas kernels for 0%

commit v1 on v0

v1 whole, which is shorter than its diff:
```python
import functools

import jax
import jax.numpy as jnp
from jax import lax
from jax.experimental import pallas as pl
from jax.experimental.pallas import tpu as pltpu
from jax.sharding import PartitionSpec as P

HEAD = 128
BLK = 128
NX = 4
SEQ = 16
GRP = 8
REP = 5
KV = 4
ROLLS = 4
SPAN = 8
D = 5120
KVW = 512
TILE = 768
DT = 640
MESH = pl.DeviceIdType.MESH
SCALE = HEAD ** (-0.5)
LOG2E = 1.4426950408889634
MASKED = -1e30
NT = (((1,), (1,)), ((), ()))
TN = (((0,), (0,)), ((), ()))
f32 = jnp.float32
bf16 = jnp.bfloat16


def vmem():
    return pl.BlockSpec(memory_space=pltpu.VMEM)


def hbm():
    return pl.BlockSpec(memory_space=pl.ANY)


def smem():
    return pl.BlockSpec(memory_space=pltpu.SMEM)


def remote(src, dst, send, recv, device):
    copy = pltpu.make_async_remote_copy(
        src_ref=src, dst_ref=dst, send_sem=send, recv_sem=recv, device_id=device, device_id_type=MESH
    )
    copy.start()
    return copy


def greet(devices):
    barrier = pltpu.get_barrier_semaphore()
    for device in devices:
        pl.semaphore_signal(barrier, inc=1, device_id=device, device_id_type=MESH)
    pl.semaphore_wait(barrier, len(devices))


def seq_peers(me):
    return [{"seq": lax.rem(me + o, SEQ)} for o in range(1, SEQ)]


def exchange_kernel(q, g, dl, k, v, qo, go, dlo, ko, vo, send_q, recv_q, send_k, recv_k, own):
    me = lax.axis_index("seq")
    x, y = me // NX, lax.rem(me, NX)
    greet(seq_peers(me))

    def cols(i, width):
        return pl.ds(pl.multiple_of(i * width, 128), width)

    copies = []
    for o in range(1, SEQ):
        d = lax.rem(me + o, SEQ)
        tx = d // NX
        for n, (src, dst) in enumerate(((k, ko), (v, vo))):
            copies.append(
                remote(src.at[:, cols(tx, HEAD)], dst.at[me], send_k.at[n, o], recv_k.at[n, o], {"seq": d})
            )
        if o % NX == 0:
            i = o // NX
            for n, (src, dst) in enumerate(((q, qo), (g, go))):
                copies.append(
                    remote(src.at[:, cols(tx, DT)], dst.at[x], send_q.at[n, i], recv_q.at[n, i], {"seq": d})
                )
            copies.append(remote(dl.at[tx], dlo.at[x], send_q.at[2, i], recv_q.at[2, i], {"seq": d}))
    mine = [
        pltpu.make_async_copy(q.at[:, cols(x, DT)], qo.at[x], own.at[0]),
        pltpu.make_async_copy(g.at[:, cols(x, DT)], go.at[x], own.at[1]),
        pltpu.make_async_copy(k.at[:, cols(x, HEAD)], ko.at[me], own.at[2]),
        pltpu.make_async_copy(v.at[:, cols(x, HEAD)], vo.at[me], own.at[3]),
        pltpu.make_async_copy(dl.at[x], dlo.at[x], own.at[4]),
    ]
    for copy in mine:
        copy.start()
    for copy in copies + mine:
        copy.wait()


def exchange(q, g, dl, k, v):
    return pl.pallas_call(
        exchange_kernel,
        out_shape=(
            jax.ShapeDtypeStruct((ROLLS, BLK, DT), bf16),
            jax.ShapeDtypeStruct((ROLLS, BLK, DT), bf16),
            jax.ShapeDtypeStruct((ROLLS, REP, BLK), f32),
            jax.ShapeDtypeStruct((SEQ, BLK, HEAD), bf16),
            jax.ShapeDtypeStruct((SEQ, BLK, HEAD), bf16),
        ),
        in_specs=[hbm()] * 5,
        out_specs=(hbm(),) * 5,
        scratch_shapes=[
            pltpu.SemaphoreType.DMA((3, NX)),
            pltpu.SemaphoreType.DMA((3, NX)),
            pltpu.SemaphoreType.DMA((2, SEQ)),
            pltpu.SemaphoreType.DMA((2, SEQ)),
            pltpu.SemaphoreType.DMA((5,)),
        ],
        compiler_params=pltpu.CompilerParams(collective_id=0, has_side_effects=True),
        name="exchange",
    )(q, g, dl, k, v)


def attention_kernel(mask, q, g, dl, k, v, pk, pv, out, s_ref, acc, qs, gs, m_ref, l_ref):
    y = lax.rem(lax.axis_index("seq"), NX)
    factor = SCALE * LOG2E
    acc[...] = jnp.zeros_like(acc)
    key_at = lax.broadcasted_iota(jnp.int32, (BLK, BLK), 0)
    query_at = lax.broadcasted_iota(jnp.int32, (BLK, BLK), 1)
    causal = key_at <= query_at

    def rollout(kk, carry):
        r = y + NX * kk
        for t in range(REP):
            qs[t] = q[kk, :, t * HEAD : (t + 1) * HEAD]
            gs[t] = g[kk, :, t * HEAD : (t + 1) * HEAD]
        m_ref[...] = jnp.full_like(m_ref, MASKED)
        l_ref[...] = jnp.zeros_like(l_ref)

        def score(slot, keys, diagonal):
            for t in range(REP):
                s = lax.dot_general(keys, qs[t], NT, preferred_element_type=f32) * factor
                if diagonal:
                    s = jnp.where(causal, s, MASKED)
                s_ref[slot, t] = s
                cut = s.reshape(BLK // 8, 8, BLK)
                before = m_ref[t]
                now = jnp.maximum(before, jnp.max(cut, axis=0))
                part = jnp.sum(jnp.exp2(cut - now[None]), axis=0)
                l_ref[t] = l_ref[t] * jnp.exp2(before - now) + part
                m_ref[t] = now

        for i in range(2):
            score(SEQ + i, pk[i], False)

        def visit(j, c):
            @pl.when(mask[r, j] == 1)
            def _():
                score(j, k[j], False)

            return c

        lax.fori_loop(0, r, visit, 0)
        score(r, k[r], True)

        lses = []
        for t in range(REP):
            top = jnp.max(m_ref[t], axis=0, keepdims=True)
            total = jnp.sum(l_ref[t] * jnp.exp2(m_ref[t] - top), axis=0, keepdims=True)
            lses.append(top + jnp.log2(total))
        for t in range(REP):
            m_ref[t] = jnp.broadcast_to(lses[t], (8, BLK))
            l_ref[t] = jnp.broadcast_to(dl[kk, t : t + 1, :], (8, BLK))

        def grads(slot, values):
            dk = jnp.zeros((BLK, HEAD), f32)
            dv = jnp.zeros((BLK, HEAD), f32)
            for t in range(REP):
                cut = s_ref[slot, t].reshape(BLK // 8, 8, BLK)
                p = jnp.exp2(cut - m_ref[t][None])
                dp = lax.dot_general(values, gs[t], NT, preferred_element_type=f32)
                ds = p * (dp.reshape(BLK // 8, 8, BLK) - l_ref[t][None])
                p = p.reshape(BLK, BLK).astype(bf16)
                ds = ds.reshape(BLK, BLK).astype(bf16)
                dk += jnp.dot(ds, qs[t], preferred_element_type=f32)
                dv += jnp.dot(p, gs[t], preferred_element_type=f32)
            acc[slot, :, 0:HEAD] += dk
            acc[slot, :, HEAD : 2 * HEAD] += dv

        for i in range(2):
            grads(SEQ + i, pv[i])

        def revisit(j, c):
            @pl.when(mask[r, j] == 1)
            def _():
                grads(j, v[j])

            return c

        lax.fori_loop(0, r + 1, revisit, 0)
        return carry

    lax.fori_loop(0, ROLLS, rollout, 0)

    for d in range(SEQ):
        rows = acc[:, d * SPAN : (d + 1) * SPAN, :]
        out[d, :, :, 0:HEAD] = (rows[:, :, 0:HEAD] * SCALE).astype(bf16)
        out[d, :, :, HEAD : 2 * HEAD] = rows[:, :, HEAD : 2 * HEAD].astype(bf16)


def attention(mask, q, g, dl, k, v, pk, pv):
    return pl.pallas_call(
        attention_kernel,
        out_shape=jax.ShapeDtypeStruct((SEQ, SEQ + 2, SPAN, 2 * HEAD), bf16),
        in_specs=[smem()] + [vmem()] * 7,
        out_specs=vmem(),
        scratch_shapes=[
            pltpu.VMEM((SEQ + 2, REP, BLK, BLK), f32),
            pltpu.VMEM((SEQ + 2, BLK, 2 * HEAD), f32),
            pltpu.VMEM((REP, BLK, HEAD), bf16),
            pltpu.VMEM((REP, BLK, HEAD), bf16),
            pltpu.VMEM((REP, 8, BLK), f32),
            pltpu.VMEM((REP, 8, BLK), f32),
        ],
        compiler_params=pltpu.CompilerParams(vmem_limit_bytes=40 * 2**20),
        name="attention",
    )(mask, q, g, dl, k, v, pk, pv)


def gather_kernel(
    listed, terms, proj, up, pair, prefix, back_r, back_p, proj_r,
    rt, pt, rp, bs, send_t, recv_t, send_j, recv_j, send_b, recv_b, send_p, recv_p,
):
    me, grp = lax.axis_index("seq"), lax.axis_index("grp")
    grp_peers = [{"grp": lax.rem(grp + i, GRP)} for i in range(1, GRP)]
    greet(seq_peers(me) + grp_peers)
    copies = []
    tree = []
    for o in range(1, SEQ):
        d = lax.rem(me + o, SEQ)
        tree.append(remote(terms.at[d], rt.at[me], send_t.at[o], recv_t.at[o], {"seq": d}))
    for o in range(1, SEQ):
        d = lax.rem(me + o, SEQ)
        copies.append(remote(proj.at[d], proj_r.at[me], send_j.at[o], recv_j.at[o], {"seq": d}))
    rt[me] = terms[me]
    proj_r[me] = proj[me]
    for copy in tree:
        copy.wait_recv()
    for h in range(KV):
        for side in range(2):
            lanes = slice(side * HEAD, (side + 1) * HEAD)
            place = slice(side * KVW + h * HEAD, side * KVW + (h + 1) * HEAD)
            for i in range(2):
                part = rt[NX * h, SEQ + i, :, lanes].astype(f32)
                for a in range(1, NX):
                    part += rt[NX * h + a, SEQ + i, :, lanes].astype(f32)
                rp[i, :, place] = part
    for b in range(GRP):
        pt[b] = rp[0] * (listed[0, 0] == b).astype(f32) + rp[1] * (listed[0, 1] == b).astype(f32)
    owners = []
    for i in range(1, GRP):
        b = lax.rem(grp + i, GRP)
        owners.append(remote(pt.at[b], rp.at[1 + i], send_p.at[i], recv_p.at[i], {"grp": b}))
    for h in range(KV):
        for side in range(2):
            lanes = slice(side * HEAD, (side + 1) * HEAD)
            place = slice(side * KVW + h * HEAD, side * KVW + (h + 1) * HEAD)
            total = rt[NX * h, 0:SEQ, :, lanes].astype(f32)
            for a in range(1, NX):
                total += rt[NX * h + a, 0:SEQ, :, lanes].astype(f32)
            pair[:, place] = total.reshape(BLK, HEAD).astype(bf16)
    back = lax.dot_general(pair[...], up[...], NT, preferred_element_type=f32)
    bs[...] = back.reshape(SEQ, SPAN, HEAD).astype(bf16)
    for o in range(1, SEQ):
        d = lax.rem(me + o, SEQ)
        copies.append(remote(bs.at[d], back_r.at[me], send_b.at[o], recv_b.at[o], {"seq": d}))
    back_r[me] = bs[me]
    for copy in owners:
        copy.wait_recv()
    total = pt[grp]
    for i in range(1, GRP):
        total += rp[1 + i]
    prefix[...] = total
    back_p[...] = lax.dot_general(total.astype(bf16), up[...], NT, preferred_element_type=f32).astype(bf16)
    for copy in tree + owners:
        copy.wait_send()
    for copy in copies:
        copy.wait()


def gather(listed, terms, proj, up):
    return pl.pallas_call(
        gather_kernel,
        out_shape=(
            jax.ShapeDtypeStruct((BLK, 2 * KVW), bf16),
            jax.ShapeDtypeStruct((SPAN, 2 * KVW), f32),
            jax.ShapeDtypeStruct((SEQ, SPAN, HEAD), bf16),
            jax.ShapeDtypeStruct((SPAN, HEAD), bf16),
            jax.ShapeDtypeStruct((SEQ, SPAN, HEAD), bf16),
        ),
        in_specs=[smem()] + [vmem()] * 3,
        out_specs=(vmem(),) * 5,
        scratch_shapes=[
            pltpu.VMEM((SEQ, SEQ + 2, SPAN, 2 * HEAD), bf16),
            pltpu.VMEM((GRP, SPAN, 2 * KVW), f32),
            pltpu.VMEM((GRP + 1, SPAN, 2 * KVW), f32),
            pltpu.VMEM((SEQ, SPAN, HEAD), bf16),
        ]
        + [pltpu.SemaphoreType.DMA((SEQ,))] * 6
        + [pltpu.SemaphoreType.DMA((GRP,))] * 2,
        compiler_params=pltpu.CompilerParams(
            collective_id=1, has_side_effects=True, vmem_limit_bytes=40 * 2**20
        ),
        name="gather",
    )(listed, terms, proj, up)


def adapters_kernel(
    back, back_p, proj, proj_p, pair, prefix, hidden, hidden_p, out,
    s0, r0, s1, r1, s2, r2, fin, a2,
    send0, recv0, send1, recv1, send2, recv2, send3, recv3, send4, recv4, send5, recv5,
):
    me, grp = lax.axis_index("seq"), lax.axis_index("grp")
    z, c = grp // 2, lax.rem(grp, 2)
    sibling = {"grp": grp + 1 - 2 * c}
    z_peers = [{"grp": lax.rem(z + i, 4) * 2 + c} for i in range(1, 4)]
    greet([sibling] + z_peers + seq_peers(me))

    back_rows = back[...].reshape(BLK, HEAD)
    back_tail = back_p[...].astype(f32)
    proj_rows = proj[...].reshape(BLK, HEAD)
    proj_tail = proj_p[...].astype(f32)
    prefix_low = prefix[...].astype(bf16).astype(f32)
    for core in range(2):
        for zz in range(4):
            b = 2 * zz + core
            cut = slice(b * DT, (b + 1) * DT)
            down = lax.dot_general(back_rows, hidden[:, cut], TN, preferred_element_type=f32)
            down += lax.dot_general(back_tail, hidden_p[:, cut].astype(f32), TN, preferred_element_type=f32)
            s0[core, zz, :, 0:DT] = down.astype(bf16)
            cut = slice(b * HEAD, (b + 1) * HEAD)
            rise = lax.dot_general(proj_rows, pair[:, cut], TN, preferred_element_type=f32)
            rise += lax.dot_general(proj_tail, prefix_low[:, cut], TN, preferred_element_type=f32)
            s0[core, zz, :, DT:TILE] = rise.astype(bf16)
    first = remote(s0.at[1 - c], r0, send0, recv0, sibling)
    first.wait_recv()
    for i in range(4):
        s1[i] = (s0[c, i].astype(f32) + r0[i].astype(f32)).astype(bf16)
    second = []
    for i in range(1, 4):
        tz = lax.rem(z + i, 4)
        second.append(remote(s1.at[tz], r1.at[i - 1], send1.at[i], recv1.at[i], {"grp": tz * 2 + c}))
    for copy in second:
        copy.wait_recv()
    total = s1[z].astype(f32)
    for i in range(3):
        total += r1[i].astype(f32)
    s2[...] = total.reshape(SEQ, SPAN, TILE).astype(bf16)
    third = []
    for o in range(1, SEQ):
        d = lax.rem(me + o, SEQ)
        third.append(remote(s2.at[d], r2.at[o], send2.at[o], recv2.at[o], {"seq": d}))
    for copy in third:
        copy.wait_recv()
    total = s2[me].astype(f32)
    for o in range(1, SEQ):
        total += r2[o].astype(f32)
    fin[...] = total.astype(bf16)
    fourth = []
    for o in range(1, SEQ):
        d = lax.rem(me + o, SEQ)
        fourth.append(remote(fin, a2.at[me], send3.at[o], recv3.at[o], {"seq": d}))
    a2[me] = fin[...]
    for copy in fourth:
        copy.wait_recv()
    fifth = []
    for i in range(1, 4):
        tz = lax.rem(z + i, 4)
        fifth.append(remote(a2, out.at[c, z], send4.at[i], recv4.at[i], {"grp": tz * 2 + c}))
    out[c, z] = a2[...]
    for copy in fifth:
        copy.wait_recv()
    sixth = remote(out.at[c], out.at[c], send5, recv5, sibling)
    sixth.wait_recv()
    for copy in [first] + second + third + fourth + fifth + [sixth]:
        copy.wait_send()


def adapters(back, back_p, proj, proj_p, pair, prefix, hidden, hidden_p):
    dma = pltpu.SemaphoreType.DMA
    return pl.pallas_call(
        adapters_kernel,
        out_shape=jax.ShapeDtypeStruct((2, 4, SEQ, SPAN, TILE), bf16),
        in_specs=[vmem()] * 8,
        out_specs=vmem(),
        scratch_shapes=[
            pltpu.VMEM((2, 4, BLK, TILE), bf16),
            pltpu.VMEM((4, BLK, TILE), bf16),
            pltpu.VMEM((4, BLK, TILE), bf16),
            pltpu.VMEM((3, BLK, TILE), bf16),
            pltpu.VMEM((SEQ, SPAN, TILE), bf16),
            pltpu.VMEM((SEQ, SPAN, TILE), bf16),
            pltpu.VMEM((SPAN, TILE), bf16),
            pltpu.VMEM((SEQ, SPAN, TILE), bf16),
            dma, dma,
            dma((4,)), dma((4,)),
            dma((SEQ,)), dma((SEQ,)),
            dma((SEQ,)), dma((SEQ,)),
            dma((4,)), dma((4,)),
            dma, dma,
        ],
        compiler_params=pltpu.CompilerParams(
            collective_id=2, has_side_effects=True, vmem_limit_bytes=48 * 2**20
        ),
        name="adapters",
    )(back, back_p, proj, proj_p, pair, prefix, hidden, hidden_p)


def on_device(
    queries, out_grad, saved_output, key_rows, value_rows, hidden_rows, prefix_keys, prefix_values,
    prefix_hidden, block_mask, prefix_list, key_down, value_down, key_up, value_up,
):
    me = lax.axis_index("seq")
    x = me // NX
    q, g = queries[0, 0], out_grad[0, 0]
    hidden = hidden_rows[0, 0]
    hidden_p = prefix_hidden[0]
    delta = jnp.sum(
        (g.astype(f32) * saved_output[0, 0].astype(f32)).reshape(BLK, KV * REP, HEAD), axis=-1
    )
    delta = delta.T.reshape(KV, REP, BLK)
    qo, go, dlo, ko, vo = exchange(q, g, delta, key_rows[0, 0], value_rows[0, 0])

    def picked(pool):
        return jnp.concatenate(
            [
                lax.dynamic_slice(pool, (prefix_list[0, i], 0, x * HEAD), (1, BLK, HEAD))
                for i in range(2)
            ]
        )

    terms = attention(
        block_mask[0], qo, go, dlo, ko, vo, picked(prefix_keys), picked(prefix_values)
    )
    down_pair = jnp.concatenate([key_down, value_down], axis=1)
    proj = jnp.dot(hidden, down_pair, preferred_element_type=f32).astype(bf16)
    proj_p = jnp.dot(hidden_p, down_pair, preferred_element_type=f32).astype(bf16)
    gap = jnp.zeros_like(key_up)
    up = jnp.concatenate(
        [jnp.concatenate([key_up, gap], axis=1), jnp.concatenate([gap, value_up], axis=1)], axis=0
    )
    pair, prefix, back_r, back_p, proj_r = gather(
        prefix_list, terms, proj.reshape(SEQ, SPAN, HEAD), up
    )
    summed = adapters(back_r, back_p, proj_r, proj_p, pair, prefix, hidden, hidden_p)
    summed = summed.reshape(2, 4, BLK, TILE)
    factor = 2.0 / (GRP * SEQ)
    down = jnp.transpose(summed[..., :DT], (2, 1, 0, 3)).reshape(2, BLK // 2, D).astype(f32) * factor
    rise = jnp.transpose(summed[..., DT:], (2, 1, 0, 3)).reshape(2, BLK // 2, 2, KVW)
    up_grads = jnp.stack([rise[0, :, 0], rise[1, :, 1]]).astype(f32) * factor
    return pair[None], prefix[None], jnp.swapaxes(down, 1, 2), up_grads


def solution(mesh):
    row = P("grp", "seq", None, None)
    in_specs = (
        row, row, row, row, row, row, P(), P(),
        P("grp", "seq", None), P("grp", None, None), P("grp", None), P(), P(), P(), P(),
    )
    out_specs = (P("grp", "seq", None), P("grp", "seq", None), P(), P())
    return jax.shard_map(
        on_device, mesh=mesh, in_specs=in_specs, out_specs=out_specs, check_vma=False
    )
```

time: 1030 us -> 167 us (0.16)
  waiting for transfers between devices: 831 us -> 0 us
  Pallas kernels: 0 us -> 141 us
  matrix products: 75.6 us -> 0.94 us
  blocking collectives: 34.3 us -> 0 us
  local copies, waits for them, and re-layouts: 39.4 us -> 18.2 us
  starting transfers between devices: 12.4 us -> 0 us
  other arithmetic: 13.9 us -> 2.05 us
    reduce_scatter x1 -> x0, waiting for transfers between devices: 580 us -> none  [on_device(): lax.psum_scatter(dense_pool, ('seq', 'grp'), scatter_dimension=0, tiled=T...]
    psum x1 -> x0, waiting for transfers between devices: 153 us -> none  [on_device(): down_grads, up_grads = lax.psum((down_terms, up_terms), ('seq', 'grp'))]
    pallas_call x0 -> x4, Pallas kernels: none -> 141 us  [the longest x1 41.5 us: adapters(): pl.pallas_call(adapters_kernel, out_shape=jax.ShapeDtypeStruct((2, 4, SEQ...]
    unnamed x5 -> x0, waiting for transfers between devices: 79.2 us -> none
    dot_general x31 -> x2, matrix products: 75.6 us -> 0.94 us  [the longest x1 0.5 us: on_device(): proj = jnp.dot(hidden, down_pair, preferred_element_type=f32).astype(bf16)]
    all_to_all x2 -> x0, blocking collectives: 34.3 us -> none  [the longest x1 19.4 us: on_device(): lax.all_to_all(by_slice(hidden_rows), 'seq', split_axis=0, concat_axis=0,...]
    all_to_all x3 -> x0, waiting for transfers between devices: 13.9 us -> none  [the longest x1 6.25 us: on_device(): lax.all_to_all(by_slice(saved_output), 'seq', split_axis=0, concat_axis=0...]
    all_to_all x3 -> x0, starting transfers between devices: 11.8 us -> none  [the longest x1 4.24 us: on_device(): lax.all_to_all(by_slice(out_grad), 'seq', split_axis=0, concat_axis=0, ti...]
  transfers between devices with their start and end apart: 7 -> 0, of which waited for: 7 -> 0; matrix products, arithmetic and copies ran while one was open for 7% -> 0% of each run, Pallas kernels for 0% -> 0%
where the time goes in v1:
time: 167 us
  Pallas kernels  141 us (84%)
  local copies, waits for them, and re-layouts  18.2 us (11%)
  between operations  4.76 us (3%)
  other arithmetic  2.05 us (1%)
    pallas_call x1, Pallas kernels, adapters(): pl.pallas_call(adapters_kernel, out_shape=jax.ShapeDtypeStruct((2, 4, SEQ...  41.5 us
    pallas_call x1, Pallas kernels, gather(): pl.pallas_call(gather_kernel, out_shape=(jax.ShapeDtypeStruct((BLK, 2 * K...  40.5 us
    pallas_call x1, Pallas kernels, exchange(): pl.pallas_call(exchange_kernel, out_shape=(jax.ShapeDtypeStruct((ROLLS, B...  33.4 us
    pallas_call x1, Pallas kernels, attention(): pl.pallas_call(attention_kernel, out_shape=jax.ShapeDtypeStruct((SEQ, SEQ...  25.3 us
    unnamed x32, local copies, waits for them, and re-layouts  9.77 us
    mul x2, local copies, waits for them, and re-layouts, on_device(): jnp.transpose(summed[..., :DT], (2, 1, 0, 3)).reshape(2, BLK // 2, D)  5.21 us

profile of v1, /device:TPU:1, one launch (start us, length us, event | category | flops | bytes accessed | tf_op | source)
XLA Modules:
  0.0 166.6 jit_solution(8278623413187775508)
XLA Ops:
  0.7 1.3 fusion.8
  5.9 0.8 constant_dynamic-slice_fusion.1
  6.7 0.9 fusion.4.up
  7.6 1.4 copy.30
  9.0 0.3 copy.29
  9.4 0.1 convert_multiply_fusion
  9.5 0.1 reduce_sum.9
  9.6 0.6 reshape.30.dl
  10.2 0.4 copy-done.10
  10.7 0.2 copy-done.11
  10.9 0.7 copy-done.5
  11.5 0.4 fusion.1.proj_p
  12.0 0.2 copy-done
  12.2 0.5 fusion.proj
  12.7 33.4 %exchange.1 = (bf16[4,128,640]{2,1,0:T(8,128)(2,1)}, bf16[4,128,640]{2,1,0:T(8,128)(2,1)}, f32[4,5,128]{2,1,0:T(8,128)}, bf16[16,128,128]{2,1,0:T(8,128)(2,1)}, bf16[16,128,128]{2,1,0:T(8,128)(2,1)}) custom-call(bf16[128,2560]{1,0:T(8,128)(2,1)} %bitcast.49, bf16[128,2560]{1,0:T(8,128)(2,1)} %bitcast.47, f32[4,5,128]{2,1,0:T(8,128)} %reshape.30.dl, ...), custom_call_target="tpu_custom_call" | custom-call | tf_op jit(solution)/shard_map/exchange/pallas_call | solution.py:101
  46.1 1.1 copy-done.1
  47.2 1.1 copy-done.2
  48.2 1.0 copy-done.3
  49.3 1.0 copy-done.4
  50.3 0.7 copy-done.6
  51.0 25.3 %attention.1.terms = bf16[16,18,8,256]{3,2,1,0:T(8,128)(2,1)S(1)} custom-call(s32[16,16]{1,0:T(8,128)S(1)} %bitcast.44, bf16[4,128,640]{2,1,0:T(8,128)(2,1)S(1)} %copy-done.1, bf16[4,128,640]{2,1,0:T(8,128)(2,1)S(1)} %copy-done.2, f32[4,5,128]{2,1,0:T(8,128)S(1)} %copy-done.6, bf16[16,128,128]{2,1,0:T(8,128)(2,1)S(1)} %copy-done.3, ...), custom_call_target="tpu_custom_call" | custom-call | tf_op jit(solution)/shard_map/attention/pallas_call | solution.py:212
  76.4 40.5 %gather.1 = (bf16[128,1024]{1,0:T(8,128)(2,1)S(1)}, f32[8,1024]{1,0:T(8,128)S(1)}, bf16[16,8,128]{2,1,0:T(8,128)(2,1)S(1)}, bf16[8,128]{1,0:T(8,128)(2,1)S(1)}, bf16[16,8,128]{2,1,0:T(8,128)(2,1)S(1)}) custom-call(s32[1,2]{1,0:T(1,128)S(1)} %copy-done.8, bf16[16,18,8,256]{3,2,1,0:T(8,128)(2,1)S(1)} %attention.1.terms, bf16[16,8,128]{2,1,0:T(8,128)(2,1)S(1)} %fusion.proj, ...), custom_call_target="tpu_custom_call" | custom-call | tf_op jit(solution)/shard_map/gather/pallas_call | solution.py:292
  116.8 41.5 %adapters.1 = bf16[2,4,16,8,768]{4,3,2,1,0:T(8,128)(2,1)S(1)} custom-call(bf16[16,8,128]{2,1,0:T(8,128)(2,1)S(1)} %get-tuple-element.21.back, bf16[8,128]{1,0:T(8,128)(2,1)S(1)} %get-tuple-element.22.back_p, bf16[16,8,128]{2,1,0:T(8,128)(2,1)S(1)} %get-tuple-element.23.proj, bf16[8,128]{1,0:T(8,128)(2,1)S(1)} %fusion.1.proj_p, ...), custom_call_target="tpu_custom_call" | custom-call | tf_op jit(solution)/shard_map/adapters/pallas_call | solution.py:391
  158.4 0.3 copy.39
  158.7 0.1 reshape.33
  158.8 0.2 fusion.7
  159.1 0.7 convert_multiply_fusion.1
  159.9 0.2 multiply_bitcast_fusion
  160.1 2.0 %copy.31 = f32[128,4,2,640]{3,2,1,0:T(2,128)S(1)} copy(f32[128,4,2,640]{3,0,1,2:T(8,128)S(1)} %multiply_bitcast_fusion) | data formatting | bytes 5242880 | tf_op jit(solution)/shard_map/mul | solution.py:458
  162.1 3.2 %mul.41 = f32[2,64,5120]{2,1,0:T(8,128)} reshape(f32[128,4,2,640]{3,2,1,0:T(2,128)S(1)} %copy.31) | data formatting | bytes 5242880 | tf_op jit(solution)/shard_map/mul | solution.py:458
  165.3 0.7 copy.45
  166.0 0.6 copy.46
  (22 shorter events, 0.2 us)
Async XLA Ops:
  0.6 8.4 %copy-start.9 = (bf16[1,1,128,2560]{3,2,1,0:T(8,128)(2,1)S(1)}, bf16[1,1,128,2560]{3,2,1,0:T(8,128)(2,1)}, u32[]{:S(2)}) copy-start(bf16[1,1,128,2560]{3,2,1,0:T(8,128)(2,1)} %param.16) | copy-start | bytes 1966084
  9.5 1.1 copy-start.10
  9.6 1.2 copy-start.11
  10.6 0.9 copy-start.5
  10.8 1.3 copy-start
  12.7 33.4 %copy-start.7 = (s32[1,16,16]{2,1,0:T(8,128)S(1)}, s32[1,16,16]{2,1,0:T(8,128)}, u32[]{:S(2)}) copy-start(s32[1,16,16]{2,1,0:T(8,128)} %param.24) | copy-start | bytes 3076
  46.1 1.1 copy-start.1
  47.2 1.1 copy-start.2
  48.2 1.0 copy-start.3
  49.3 1.0 copy-start.4
  50.3 0.7 copy-start.6
  51.0 25.3 %copy-start.8 = (s32[1,2]{1,0:T(1,128)S(1)}, s32[1,2]{1,0:T(1,128)}, u32[]{:S(2)}) copy-start(s32[1,2]{1,0:T(1,128)} %listed.1) | copy-start | bytes 28

commit v2 on v1

v2 whole, which is shorter than its diff:
```python
import jax
import jax.numpy as jnp
from jax import lax
from jax.experimental import pallas as pl
from jax.experimental.pallas import tpu as pltpu
from jax.sharding import PartitionSpec as P

HEAD = 128
BLK = 128
NX = 4
SEQ = 16
GRP = 8
REP = 5
KV = 4
SPAN = 8
D = 5120
KVW = 512
DT = 640
TILE = DT + HEAD
W = REP * BLK
TREE = SEQ * BLK
GROUP = 4 * BLK
PAIR = 2 * HEAD
CHUNKS = ((0, 256), (256, 512), (512, 640))
MESH = pl.DeviceIdType.MESH
SCALE = HEAD ** (-0.5)
LOG2E = 1.4426950408889634
MASKED = -1e30
NT = (((1,), (1,)), ((), ()))
TN = (((0,), (0,)), ((), ()))
f32 = jnp.float32
bf16 = jnp.bfloat16


def vmem():
    return pl.BlockSpec(memory_space=pltpu.VMEM)


def hbm():
    return pl.BlockSpec(memory_space=pl.ANY)


def smem():
    return pl.BlockSpec(memory_space=pltpu.SMEM)


def remote(src, dst, send, recv, device):
    copy = pltpu.make_async_remote_copy(
        src_ref=src, dst_ref=dst, send_sem=send, recv_sem=recv, device_id=device, device_id_type=MESH
    )
    copy.start()
    return copy


def greet(devices):
    barrier = pltpu.get_barrier_semaphore()
    for device in devices:
        pl.semaphore_signal(barrier, inc=1, device_id=device, device_id_type=MESH)
    pl.semaphore_wait(barrier, len(devices))


def cols(i, width):
    return pl.ds(pl.multiple_of(i * width, 128), width)


def rows(i, count):
    return pl.ds(pl.multiple_of(i * count, count), count)


def kernel(
    mask, listed, q, g, saved, k, v, hidden, hidden_p, pool_k, pool_v, down_k, down_v, up_k, up_v,
    pair, prefix, out,
    q_in, g_in, delta_in, kv, own_g, own_s, own_h, own_p, down, pool, up, delta_out,
    s_ref, acc, qs, gs, pb, dsb, top, low, diag,
    tsend, rt, proj_s, proj_r, pt, rp, back_s, back_r,
    s0, r0, s1, r1, s2, r2, fin, a2,
    sem_in, kvx_s, kvx_r, kvy_s, kvy_r, q_s, q_r, t_s, t_r, j_s, j_r, b_s, b_r, p_s, p_r,
    s0_s, s0_r, s1_s, s1_r, s2_s, s2_r, a2_s, a2_r, a1_s, a1_r, a0_s, a0_r,
):
    me, grp = lax.axis_index("seq"), lax.axis_index("grp")
    x, y = me // NX, lax.rem(me, NX)
    z, c = grp // 2, lax.rem(grp, 2)
    peers = [lax.rem(me + o, SEQ) for o in range(1, SEQ)]

    def local(src, dst, i):
        copy = pltpu.make_async_copy(src, dst, sem_in.at[i])
        copy.start()
        return copy

    mine = rows(me, BLK)
    keep = [
        local(k.at[:, cols(x, HEAD)], kv.at[mine, 0:HEAD], 0),
        local(v.at[:, cols(x, HEAD)], kv.at[mine, HEAD:PAIR], 1),
        local(q.at[:, cols(x, DT)], q_in.at[x], 2),
        local(g.at[:, cols(x, DT)], g_in.at[x], 3),
        local(g, own_g, 4),
        local(saved, own_s, 5),
        local(hidden, own_h, 6),
        local(down_k, down.at[0:64], 7),
        local(down_v, down.at[64:128], 8),
        local(hidden_p, own_p, 9),
        local(pool_k.at[:, :, cols(x, HEAD)], pool.at[:, :, 0:HEAD], 10),
        local(pool_v.at[:, :, cols(x, HEAD)], pool.at[:, :, HEAD:PAIR], 11),
    ]
    greet([{"seq": d} for d in peers] + [{"grp": lax.rem(grp + i, GRP)} for i in range(1, GRP)])

    step_x = []
    for i in range(1, NX):
        tx = lax.rem(x + i, NX)
        device = {"seq": tx * NX + y}
        step_x.append(
            (
                remote(k.at[:, cols(tx, HEAD)], kv.at[mine, 0:HEAD], kvx_s.at[0, i], kvx_r.at[0, i], device),
                remote(v.at[:, cols(tx, HEAD)], kv.at[mine, HEAD:PAIR], kvx_s.at[1, i], kvx_r.at[1, i], device),
            )
        )
    step_q = []
    for i in range(1, NX):
        tx = lax.rem(x + i, NX)
        device = {"seq": tx * NX + y}
        step_q.append(remote(q.at[:, cols(tx, DT)], q_in.at[x], q_s.at[0, i], q_r.at[0, i], device))
        step_q.append(remote(g.at[:, cols(tx, DT)], g_in.at[x], q_s.at[1, i], q_r.at[1, i], device))
    keep[0].wait()
    keep[1].wait()
    step_y = []
    for n in range(NX):
        if n:
            for copy in step_x[n - 1]:
                copy.wait_recv()
        block = rows(lax.rem(x + NX - n, NX) * NX + y, BLK)
        for i in range(1, NX):
            device = {"seq": x * NX + lax.rem(y + i, NX)}
            step_y.append(remote(kv.at[block], kv.at[block], kvy_s.at[n, i], kvy_r.at[n, i], device))

    keep[4].wait()
    keep[5].wait()
    ones = jnp.ones((8, HEAD), f32)
    for h in range(KV):
        for t in range(REP):
            cut = slice((h * REP + t) * HEAD, (h * REP + t + 1) * HEAD)
            prod = own_g[:, cut].astype(f32) * own_s[:, cut].astype(f32)
            delta_out[h, :, t * BLK : (t + 1) * BLK] = lax.dot_general(
                ones, prod, NT, preferred_element_type=f32, precision=lax.Precision.HIGHEST
            )
    for i in range(1, NX):
        tx = lax.rem(x + i, NX)
        step_q.append(
            remote(delta_out.at[tx], delta_in.at[x], q_s.at[2, i], q_r.at[2, i], {"seq": tx * NX + y})
        )
    delta_in[x] = delta_out[x]

    for i in range(6, 10):
        keep[i].wait()
    proj = lax.dot_general(own_h[...], down[...], NT, preferred_element_type=f32)
    proj_s[...] = proj.reshape(SEQ, SPAN, HEAD).astype(bf16)
    step_j = []
    for o, d in enumerate(peers):
        step_j.append(remote(proj_s.at[d], proj_r.at[me], j_s.at[o], j_r.at[o], {"seq": d}))
    proj_r[me] = proj_s[me]
    proj_tail = lax.dot_general(own_p[...], down[...], NT, preferred_element_type=f32).astype(bf16)
    up[...] = jnp.zeros_like(up)
    up[0:64, 0:KVW] = up_k[...]
    up[64:128, KVW : 2 * KVW] = up_v[...]

    keep[10].wait()
    keep[11].wait()
    for i in range(2):
        kv[TREE + i * BLK : TREE + (i + 1) * BLK, :] = pool[listed[0, i]]
    acc[...] = jnp.zeros_like(acc)
    key_at = lax.broadcasted_iota(jnp.int32, (GROUP, BLK), 0)
    query_at = lax.broadcasted_iota(jnp.int32, (GROUP, BLK), 1)
    diag[...] = jnp.where(key_at <= y * BLK + query_at, 0.0, MASKED).astype(f32)
    keep[2].wait()
    keep[3].wait()
    for copy in step_q + step_y:
        copy.wait_recv()

    def rollout(step, carry):
        kk = NX - 1 - step
        r = y + NX * kk
        for t in range(REP):
            span = slice(t * BLK, (t + 1) * BLK)
            qs[span, :] = q_in[kk, :, span]
            gs[span, :] = g_in[kk, :, span]
        top[...] = jnp.full_like(top, MASKED)
        low[...] = jnp.zeros_like(low)

        def hides(m):
            return [(mask[r, m * 4 + b].astype(f32) - 1.0) * 1e30 for b in range(4)]

        def score(place, hidden_by, diagonal, n):
            for lo, hi in CHUNKS:
                w = hi - lo
                s = lax.dot_general(kv[place, 0:HEAD], qs[lo:hi, :], NT, preferred_element_type=f32)
                s = s * (SCALE * LOG2E)
                if diagonal:
                    s = s + jnp.concatenate([diag[...]] * (w // BLK), axis=1)
                s_ref[place, lo:hi] = s
                cut = s.reshape(n, BLK // 8, 8, w)
                before = top[:, lo:hi]
                now = before
                for b in range(n):
                    now = jnp.maximum(now, jnp.max(cut[b], axis=0) + hidden_by[b])
                part = low[:, lo:hi] * jnp.exp2(before - now)
                for b in range(n):
                    part += jnp.sum(jnp.exp2(cut[b] - (now - hidden_by[b])[None]), axis=0)
                low[:, lo:hi] = part
                top[:, lo:hi] = now

        def score_group(m, cc):
            score(rows(m, GROUP), hides(m), False, 4)
            return cc

        ends = slice(TREE, TREE + 2 * BLK)
        score(ends, [0.0, 0.0], False, 2)
        lax.fori_loop(0, kk, score_group, 0)
        score(rows(kk, GROUP), hides(kk), True, 4)
        best = jnp.max(top[...], axis=0, keepdims=True)
        total = jnp.sum(low[...] * jnp.exp2(top[...] - best), axis=0, keepdims=True)
        top[...] = jnp.broadcast_to(best + jnp.log2(total), (8, W))
        low[...] = delta_in[kk]

        def grads(place, hidden_by, n):
            for lo, hi in CHUNKS:
                w = hi - lo
                dp = lax.dot_general(kv[place, HEAD:PAIR], gs[lo:hi, :], NT, preferred_element_type=f32)
                dp = dp.reshape(n, BLK // 8, 8, w)
                cut = s_ref[place, lo:hi].reshape(n, BLK // 8, 8, w)
                for b in range(n):
                    span = slice(b * BLK, (b + 1) * BLK)
                    p = jnp.exp2(cut[b] - (top[:, lo:hi] - hidden_by[b])[None])
                    ds = p * (dp[b] - low[:, lo:hi][None])
                    pb[span, lo:hi] = p.reshape(BLK, w).astype(bf16)
                    dsb[span, lo:hi] = ds.reshape(BLK, w).astype(bf16)
            acc[place, 0:HEAD] += jnp.dot(dsb[0 : n * BLK, :], qs[...], preferred_element_type=f32)
            acc[place, HEAD:PAIR] += jnp.dot(pb[0 : n * BLK, :], gs[...], preferred_element_type=f32)

        def grads_group(m, cc):
            grads(rows(m, GROUP), hides(m), 4)
            return cc

        grads(ends, [0.0, 0.0], 2)
        lax.fori_loop(0, kk + 1, grads_group, 0)

        for b in range(4):
            j = kk * 4 + b
            part = acc[rows(j, BLK), :].reshape(SEQ, SPAN, PAIR)
            tsend[:, j, :, 0:HEAD] = (part[:, :, 0:HEAD] * SCALE).astype(bf16)
            tsend[:, j, :, HEAD:PAIR] = part[:, :, HEAD:PAIR].astype(bf16)

        @pl.when(step < NX - 1)
        def _():
            for o, d in enumerate(peers):
                four = pl.ds(kk * 4, 4)
                remote(tsend.at[d, four], rt.at[me, four], t_s.at[kk, o], t_r.at[kk, o], {"seq": d})

        return carry

    lax.fori_loop(0, NX, rollout, 0)
    for i in range(2):
        part = acc[TREE + i * BLK : TREE + (i + 1) * BLK, :].reshape(SEQ, SPAN, PAIR)
        tsend[:, SEQ + i, :, 0:HEAD] = (part[:, :, 0:HEAD] * SCALE).astype(bf16)
        tsend[:, SEQ + i, :, HEAD:PAIR] = part[:, :, HEAD:PAIR].astype(bf16)
    step_e = []
    two = pl.ds(SEQ, 2)
    for o, d in enumerate(peers):
        step_e.append(remote(tsend.at[d, two], rt.at[me, two], t_s.at[4, o], t_r.at[4, o], {"seq": d}))
    step_t = []
    for kk in range(NX):
        four = pl.ds(kk * 4, 4)
        for o, d in enumerate(peers):
            copy = pltpu.make_async_remote_copy(
                src_ref=tsend.at[d, four], dst_ref=rt.at[me, four], send_sem=t_s.at[kk, o],
                recv_sem=t_r.at[kk, o], device_id={"seq": d}, device_id_type=MESH,
            )
            if kk == 0:
                copy.start()
            step_t.append(copy)
    rt[me] = tsend[me]
    for copy in step_e:
        copy.wait_recv()
    for h in range(KV):
        for side in range(2):
            lanes = slice(side * HEAD, (side + 1) * HEAD)
            place = slice(side * KVW + h * HEAD, side * KVW + (h + 1) * HEAD)
            for i in range(2):
                part = rt[NX * h, SEQ + i, :, lanes].astype(f32)
                for a in range(1, NX):
                    part += rt[NX * h + a, SEQ + i, :, lanes].astype(f32)
                rp[i, :, place] = part
    for b in range(GRP):
        pt[b] = rp[0] * (listed[0, 0] == b).astype(f32) + rp[1] * (listed[0, 1] == b).astype(f32)
    step_p = []
    for i in range(1, GRP):
        b = lax.rem(grp + i, GRP)
        step_p.append(remote(pt.at[b], rp.at[1 + i], p_s.at[i], p_r.at[i], {"grp": b}))
    for copy in step_t:
        copy.wait_recv()
    for h in range(KV):
        for side in range(2):
            lanes = slice(side * HEAD, (side + 1) * HEAD)
            place = slice(side * KVW + h * HEAD, side * KVW + (h + 1) * HEAD)
            total = rt[NX * h, 0:SEQ, :, lanes].astype(f32)
            for a in range(1, NX):
                total += rt[NX * h + a, 0:SEQ, :, lanes].astype(f32)
            pair[:, place] = total.reshape(BLK, HEAD).astype(bf16)
    back = lax.dot_general(pair[...], up[...], NT, preferred_element_type=f32)
    back_s[...] = back.reshape(SEQ, SPAN, HEAD).astype(bf16)
    step_b = []
    for o, d in enumerate(peers):
        step_b.append(remote(back_s.at[d], back_r.at[me], b_s.at[o], b_r.at[o], {"seq": d}))
    back_r[me] = back_s[me]
    for copy in step_p:
        copy.wait_recv()
    total = pt[grp]
    for i in range(1, GRP):
        total += rp[1 + i]
    prefix[...] = total
    prefix_low = total.astype(bf16)
    back_tail = lax.dot_general(prefix_low, up[...], NT, preferred_element_type=f32).astype(bf16)
    for copy in step_j:
        copy.wait_recv()
    proj_rows = proj_r[...].reshape(BLK, HEAD)
    proj_tail = proj_tail.astype(f32)
    prefix_low = prefix_low.astype(f32)
    for b in range(GRP):
        cut = slice(b * HEAD, (b + 1) * HEAD)
        rise = lax.dot_general(proj_rows, pair[:, cut], TN, preferred_element_type=f32)
        rise += lax.dot_general(proj_tail, prefix_low[:, cut], TN, preferred_element_type=f32)
        s0[b % 2, b // 2, :, DT:TILE] = rise.astype(bf16)
    for copy in step_b:
        copy.wait_recv()

    back_rows = back_r[...].reshape(BLK, HEAD)
    back_tail = back_tail.astype(f32)
    for b in range(GRP):
        cut = slice(b * DT, (b + 1) * DT)
        part = lax.dot_general(back_rows, own_h[:, cut], TN, preferred_element_type=f32)
        part += lax.dot_general(back_tail, own_p[:, cut].astype(f32), TN, preferred_element_type=f32)
        s0[b % 2, b // 2, :, 0:DT] = part.astype(bf16)
    sibling = {"grp": grp + 1 - 2 * c}
    first = remote(s0.at[1 - c], r0, s0_s, s0_r, sibling)
    first.wait_recv()
    for i in range(4):
        s1[i] = (s0[c, i].astype(f32) + r0[i].astype(f32)).astype(bf16)
    second = []
    for i in range(1, 4):
        tz = lax.rem(z + i, 4)
        second.append(remote(s1.at[tz], r1.at[i - 1], s1_s.at[i], s1_r.at[i], {"grp": tz * 2 + c}))
    for copy in second:
        copy.wait_recv()
    total = s1[z].astype(f32)
    for i in range(3):
        total += r1[i].astype(f32)
    s2[...] = total.reshape(SEQ, SPAN, TILE).astype(bf16)
    third = []
    for o, d in enumerate(peers):
        third.append(remote(s2.at[d], r2.at[o], s2_s.at[o], s2_r.at[o], {"seq": d}))
    for copy in third:
        copy.wait_recv()
    total = s2[me].astype(f32)
    for o in range(SEQ - 1):
        total += r2[o].astype(f32)
    fin[...] = total.astype(bf16)
    fourth = []
    for o, d in enumerate(peers):
        fourth.append(remote(fin, a2.at[me], a2_s.at[o], a2_r.at[o], {"seq": d}))
    a2[me] = fin[...]
    for copy in fourth:
        copy.wait_recv()
    fifth = []
    for i in range(1, 4):
        tz = lax.rem(z + i, 4)
        fifth.append(remote(a2, out.at[c, z], a1_s.at[i], a1_r.at[i], {"grp": tz * 2 + c}))
    out[c, z] = a2[...]
    for copy in fifth:
        copy.wait_recv()
    sixth = remote(out.at[c], out.at[c], a0_s, a0_r, sibling)
    sixth.wait_recv()

    for pairs in step_x:
        for copy in pairs:
            copy.wait_send()
    for copy in (
        step_q + step_y + step_j + step_e + step_t + step_p + step_b
        + [first] + second + third + fourth + fifth + [sixth]
    ):
        copy.wait_send()


def backward(*operands):
    dma = pltpu.SemaphoreType.DMA

    def low(*shape):
        return pltpu.VMEM(shape, bf16)

    def wide(*shape):
        return pltpu.VMEM(shape, f32)

    return pl.pallas_call(
        kernel,
        out_shape=(
            jax.ShapeDtypeStruct((BLK, 2 * KVW), bf16),
            jax.ShapeDtypeStruct((SPAN, 2 * KVW), f32),
            jax.ShapeDtypeStruct((2, 4, SEQ, SPAN, TILE), bf16),
        ),
        in_specs=[smem()] * 2 + [hbm()] * 11 + [vmem()] * 2,
        out_specs=(vmem(),) * 3,
        scratch_shapes=[
            low(NX, BLK, DT), low(NX, BLK, DT), wide(NX, 8, W), low(TREE + 2 * BLK, PAIR),
            low(BLK, 4 * DT), low(BLK, 4 * DT), low(BLK, D), low(SPAN, D), low(HEAD, D),
            low(GRP, BLK, PAIR), low(HEAD, 2 * KVW), wide(KV, 8, W),
            wide(TREE + 2 * BLK, W), wide(TREE + 2 * BLK, PAIR), low(W, HEAD), low(W, HEAD),
            low(GROUP, W), low(GROUP, W), wide(8, W), wide(8, W), wide(GROUP, BLK),
            low(SEQ, SEQ + 2, SPAN, PAIR), low(SEQ, SEQ + 2, SPAN, PAIR),
            low(SEQ, SPAN, HEAD), low(SEQ, SPAN, HEAD),
            wide(GRP, SPAN, 2 * KVW), wide(GRP + 1, SPAN, 2 * KVW),
            low(SEQ, SPAN, HEAD), low(SEQ, SPAN, HEAD),
            low(2, 4, BLK, TILE), low(4, BLK, TILE), low(4, BLK, TILE), low(3, BLK, TILE),
            low(SEQ, SPAN, TILE), low(SEQ, SPAN, TILE), low(SPAN, TILE), low(SEQ, SPAN, TILE),
            dma((12,)),
            dma((2, NX)), dma((2, NX)), dma((NX, NX)), dma((NX, NX)), dma((3, NX)), dma((3, NX)),
            dma((5, SEQ)), dma((5, SEQ)), dma((SEQ,)), dma((SEQ,)), dma((SEQ,)), dma((SEQ,)),
            dma((GRP,)), dma((GRP,)),
            dma, dma, dma((4,)), dma((4,)), dma((SEQ,)), dma((SEQ,)), dma((SEQ,)), dma((SEQ,)),
            dma((4,)), dma((4,)), dma, dma,
        ],
        compiler_params=pltpu.CompilerParams(
            collective_id=0, has_side_effects=True, vmem_limit_bytes=56 * 2**20
        ),
        name="backward",
    )(*operands)


def spread_kernel(summed, down, rise):
    factor = 2.0 / (GRP * SEQ)
    b = pl.program_id(0)
    part = summed[0, 0].reshape(BLK, TILE).astype(f32) * factor
    down[...] = part[:, 0:DT]
    rise[0] = jnp.where(b < 4, part[0:64, DT:TILE], part[64:128, DT:TILE])


def spread(summed):
    return pl.pallas_call(
        spread_kernel,
        grid=(GRP,),
        out_shape=(
            jax.ShapeDtypeStruct((BLK, D), f32),
            jax.ShapeDtypeStruct((2, 64, KVW), f32),
        ),
        in_specs=[pl.BlockSpec((1, 1, SEQ, SPAN, TILE), lambda b: (b % 2, b // 2, 0, 0, 0))],
        out_specs=(
            pl.BlockSpec((BLK, DT), lambda b: (0, b)),
            pl.BlockSpec((1, 64, HEAD), lambda b: (b // 4, 0, b % 4)),
        ),
        name="spread",
    )(summed)


def on_device(
    queries, out_grad, saved_output, key_rows, value_rows, hidden_rows, prefix_keys, prefix_values,
    prefix_hidden, block_mask, prefix_list, key_down, value_down, key_up, value_up,
):
    pair, prefix, summed = backward(
        block_mask[0], prefix_list, queries[0, 0], out_grad[0, 0], saved_output[0, 0],
        key_rows[0, 0], value_rows[0, 0], hidden_rows[0, 0], prefix_hidden[0],
        prefix_keys, prefix_values, key_down.T, value_down.T, key_up, value_up,
    )
    down, rise = spread(summed)
    down = jnp.swapaxes(down.reshape(2, BLK // 2, D), 1, 2)
    return pair[None], prefix[None], down, rise


def solution(mesh):
    row = P("grp", "seq", None, None)
    in_specs = (
        row, row, row, row, row, row, P(), P(),
        P("grp", "seq", None), P("grp", None, None), P("grp", None), P(), P(), P(), P(),
    )
    out_specs = (P("grp", "seq", None), P("grp", "seq", None), P(), P())
    return jax.shard_map(
        on_device, mesh=mesh, in_specs=in_specs, out_specs=out_specs, check_vma=False
    )
```

time: 167 us -> 110 us (0.66)
  Pallas kernels: 141 us -> 107 us
  local copies, waits for them, and re-layouts: 18.2 us -> 1.33 us
  between operations: 4.76 us -> 0.66 us
  other arithmetic: 2.05 us -> 0 us
    pallas_call x4 -> x2, Pallas kernels: 141 us -> 107 us  [the longest x1 102 us: backward(): pl.pallas_call(kernel, out_shape=(jax.ShapeDtypeStruct((BLK, 2 * KVW), bf...]
    unnamed x32 -> x6, local copies, waits for them, and re-layouts: 9.77 us -> 1.33 us
    mul x2 -> x0, local copies, waits for them, and re-layouts: 5.21 us -> none  [on_device(): jnp.transpose(summed[..., :DT], (2, 1, 0, 3)).reshape(2, BLK // 2, D)]
where the time goes in v2:
time: 110 us; the launch traced here: 109 us
  Pallas kernels  107 us (97%)
  local copies, waits for them, and re-layouts  1.33 us (1%)
    pallas_call x1, Pallas kernels, backward(): pl.pallas_call(kernel, out_shape=(jax.ShapeDtypeStruct((BLK, 2 * KVW), bf...  102 us
    pallas_call x1, Pallas kernels, spread(): pl.pallas_call(spread_kernel, grid=(GRP,), out_shape=(jax.ShapeDtypeStruc...  5.81 us

profile of v2, /device:TPU:1, one launch (start us, length us, event | category | flops | bytes accessed | tf_op | source)
XLA Modules:
  0.0 109.3 jit_solution(18172089114663661119)
XLA Ops:
  0.6 101.5 %backward.1 = (bf16[128,1024]{1,0:T(8,128)(2,1)}, f32[8,1024]{1,0:T(8,128)}, bf16[2,4,16,8,768]{4,3,2,1,0:T(8,128)(2,1)}) custom-call(s32[16,16]{1,0:T(8,128)} %bitcast.26, s32[1,2]{1,0:T(1,128)} %listed.1, bf16[128,2560]{1,0:T(8,128)(2,1)} %bitcast.16, bf16[128,2560]{1,0:T(8,128)(2,1)} %bitcast.17, bf16[128,2560]{1,0:T(8,128)(2,1)} %bitcast.18, ...), custom_call_target="tpu_custom_call" | custom-call | tf_op jit(solution)/shard_map/backward/pallas_call | solution.py:400
  102.2 0.0 copy-start
  102.2 0.0 copy-start.1
  102.2 5.8 %spread.1 = (f32[128,5120]{1,0:T(8,128)}, f32[2,64,512]{2,1,0:T(8,128)}) custom-call(bf16[2,4,16,8,768]{4,3,2,1,0:T(8,128)(2,1)} %get-tuple-element.11.summed), custom_call_target="tpu_custom_call" | custom-call | tf_op jit(solution)/shard_map/spread/pallas_call | solution.py:444
  108.0 0.0 copy-done
  108.0 0.7 copy.21
  108.7 0.0 copy-done.1
  108.7 0.6 copy.22
Async XLA Ops:
  102.2 5.8 %copy-start = (bf16[128,1024]{1,0:T(8,128)(2,1)S(1)}, bf16[128,1024]{1,0:T(8,128)(2,1)}, u32[]{:S(2)}) copy-start(bf16[128,1024]{1,0:T(8,128)(2,1)} %get-tuple-element.9) | copy-start | bytes 786436
  102.2 6.5 %copy-start.1 = (f32[8,1024]{1,0:T(8,128)S(1)}, f32[8,1024]{1,0:T(8,128)}, u32[]{:S(2)}) copy-start(f32[8,1024]{1,0:T(8,128)} %get-tuple-element.10) | copy-start | bytes 98308

commit v3 on v2

--- a/solution.py
+++ b/solution.py
@@ -16,7 +16,9 @@
 D = 5120
 KVW = 512
 DT = 640
-TILE = DT + HEAD
+TILE = 256
+DEPTH = 144
+TYPES = 3
 W = REP * BLK
 TREE = SEQ * BLK
 GROUP = 4 * BLK
@@ -56,7 +58,10 @@
     barrier = pltpu.get_barrier_semaphore()
     for device in devices:
         pl.semaphore_signal(barrier, inc=1, device_id=device, device_id_type=MESH)
-    pl.semaphore_wait(barrier, len(devices))
+
+
+def greeted(devices):
+    pl.semaphore_wait(pltpu.get_barrier_semaphore(), len(devices))
 
 
 def cols(i, width):
@@ -70,10 +75,10 @@
 def kernel(
     mask, listed, q, g, saved, k, v, hidden, hidden_p, pool_k, pool_v, down_k, down_v, up_k, up_v,
     pair, prefix, out,
-    q_in, g_in, delta_in, kv, own_g, own_s, own_h, own_p, down, pool, up, delta_out,
+    q_in, g_in, delta_in, kv, own_g, own_s, own_h, own_p, down, pool, up, delta_out, all_g, back_all, back_t, proj_all, proj_t,
     s_ref, acc, qs, gs, pb, dsb, top, low, diag,
     tsend, rt, proj_s, proj_r, pt, rp, back_s, back_r,
-    s0, r0, s1, r1, s2, r2, fin, a2,
+    s0, r0, s1, r1, s2, r2,
     sem_in, kvx_s, kvx_r, kvy_s, kvy_r, q_s, q_r, t_s, t_r, j_s, j_r, b_s, b_r, p_s, p_r,
     s0_s, s0_r, s1_s, s1_r, s2_s, s2_r, a2_s, a2_r, a1_s, a1_r, a0_s, a0_r,
 ):
@@ -81,6 +86,27 @@
     x, y = me // NX, lax.rem(me, NX)
     z, c = grp // 2, lax.rem(grp, 2)
     peers = [lax.rem(me + o, SEQ) for o in range(1, SEQ)]
+
+    def at(xx, yy, zz):
+        return {"seq": xx * NX + yy, "grp": zz * 2 + c}
+
+    def line(t, i):
+        n = [lax.rem(place + i, NX) for place in (z, x, y)]
+        return (at(x, y, n[0]), at(n[1], y, z), at(x, n[2], z))[t]
+
+    def plane(t, e):
+        u, w = e // NX, lax.rem(e, NX)
+        return (at(u, w, z), at(x, u, w), at(u, y, w))[t]
+
+    on_line = (z, x, y)
+    on_plane = (me, y * NX + z, x * NX + z)
+    met = [{"grp": lax.rem(grp + i, GRP)} for i in range(1, GRP)]
+    met += [{"seq": d} for d in peers]
+    for i in range(1, NX):
+        for j in range(1, NX):
+            met.append(at(x, lax.rem(y + i, NX), lax.rem(z + j, NX)))
+            met.append(at(lax.rem(x + i, NX), y, lax.rem(z + j, NX)))
+    greet(met)
 
     def local(src, dst, i):
         copy = pltpu.make_async_copy(src, dst, sem_in.at[i])
@@ -95,14 +121,25 @@
         local(g.at[:, cols(x, DT)], g_in.at[x], 3),
         local(g, own_g, 4),
         local(saved, own_s, 5),
-        local(hidden, own_h, 6),
+        local(hidden, own_h.at[0:BLK], 6),
         local(down_k, down.at[0:64], 7),
         local(down_v, down.at[64:128], 8),
         local(hidden_p, own_p, 9),
         local(pool_k.at[:, :, cols(x, HEAD)], pool.at[:, :, 0:HEAD], 10),
         local(pool_v.at[:, :, cols(x, HEAD)], pool.at[:, :, HEAD:PAIR], 11),
     ]
-    greet([{"seq": d} for d in peers] + [{"grp": lax.rem(grp + i, GRP)} for i in range(1, GRP)])
+    keep[4].wait()
+    keep[5].wait()
+    ones = jnp.ones((8, HEAD), f32)
+    for h in range(KV):
+        for t in range(REP):
+            cut = slice((h * REP + t) * HEAD, (h * REP + t + 1) * HEAD)
+            prod = own_g[:, cut].astype(f32) * own_s[:, cut].astype(f32)
+            delta_out[h, :, t * BLK : (t + 1) * BLK] = lax.dot_general(
+                ones, prod, NT, preferred_element_type=f32, precision=lax.Precision.HIGHEST
+            )
+    delta_in[x] = delta_out[x]
+    greeted(met)
 
     step_x = []
     for i in range(1, NX):
@@ -114,50 +151,43 @@
                 remote(v.at[:, cols(tx, HEAD)], kv.at[mine, HEAD:PAIR], kvx_s.at[1, i], kvx_r.at[1, i], device),
             )
         )
+    keep[0].wait()
+    keep[1].wait()
+    step_y = []
+
+    def forward(n):
+        block = rows(lax.rem(x + NX - n, NX) * NX + y, BLK)
+        for i in range(1, NX):
+            device = {"seq": x * NX + lax.rem(y + i, NX)}
+            step_y.append(remote(kv.at[block], kv.at[block], kvy_s.at[n, i], kvy_r.at[n, i], device))
+
+    forward(0)
     step_q = []
+    for i in range(1, NX):
+        tx = lax.rem(x + i, NX)
+        device = {"seq": tx * NX + y}
+        step_q.append(remote(delta_out.at[tx], delta_in.at[x], q_s.at[2, i], q_r.at[2, i], device))
     for i in range(1, NX):
         tx = lax.rem(x + i, NX)
         device = {"seq": tx * NX + y}
         step_q.append(remote(q.at[:, cols(tx, DT)], q_in.at[x], q_s.at[0, i], q_r.at[0, i], device))
         step_q.append(remote(g.at[:, cols(tx, DT)], g_in.at[x], q_s.at[1, i], q_r.at[1, i], device))
-    keep[0].wait()
-    keep[1].wait()
-    step_y = []
-    for n in range(NX):
-        if n:
-            for copy in step_x[n - 1]:
-                copy.wait_recv()
-        block = rows(lax.rem(x + NX - n, NX) * NX + y, BLK)
-        for i in range(1, NX):
-            device = {"seq": x * NX + lax.rem(y + i, NX)}
-            step_y.append(remote(kv.at[block], kv.at[block], kvy_s.at[n, i], kvy_r.at[n, i], device))
-
-    keep[4].wait()
-    keep[5].wait()
-    ones = jnp.ones((8, HEAD), f32)
-    for h in range(KV):
-        for t in range(REP):
-            cut = slice((h * REP + t) * HEAD, (h * REP + t + 1) * HEAD)
-            prod = own_g[:, cut].astype(f32) * own_s[:, cut].astype(f32)
-            delta_out[h, :, t * BLK : (t + 1) * BLK] = lax.dot_general(
-                ones, prod, NT, preferred_element_type=f32, precision=lax.Precision.HIGHEST
-            )
-    for i in range(1, NX):
-        tx = lax.rem(x + i, NX)
-        step_q.append(
-            remote(delta_out.at[tx], delta_in.at[x], q_s.at[2, i], q_r.at[2, i], {"seq": tx * NX + y})
-        )
-    delta_in[x] = delta_out[x]
+    for n in (1, 3, 2):
+        for copy in step_x[n - 1]:
+            copy.wait_recv()
+        forward(n)
 
     for i in range(6, 10):
         keep[i].wait()
+    own_h[BLK : BLK + SPAN, :] = own_p[...]
+    own_h[BLK + SPAN : DEPTH, :] = jnp.zeros((SPAN, D), bf16)
     proj = lax.dot_general(own_h[...], down[...], NT, preferred_element_type=f32)
-    proj_s[...] = proj.reshape(SEQ, SPAN, HEAD).astype(bf16)
+    proj_s[...] = proj[0:BLK].reshape(SEQ, SPAN, HEAD).astype(bf16)
+    proj_all[BLK:DEPTH, :] = proj[BLK:DEPTH].astype(bf16)
     step_j = []
     for o, d in enumerate(peers):
         step_j.append(remote(proj_s.at[d], proj_r.at[me], j_s.at[o], j_r.at[o], {"seq": d}))
     proj_r[me] = proj_s[me]
-    proj_tail = lax.dot_general(own_p[...], down[...], NT, preferred_element_type=f32).astype(bf16)
     up[...] = jnp.zeros_like(up)
     up[0:64, 0:KVW] = up_k[...]
     up[64:128, KVW : 2 * KVW] = up_v[...]
@@ -303,8 +333,8 @@
             total = rt[NX * h, 0:SEQ, :, lanes].astype(f32)
             for a in range(1, NX):
                 total += rt[NX * h + a, 0:SEQ, :, lanes].astype(f32)
-            pair[:, place] = total.reshape(BLK, HEAD).astype(bf16)
-    back = lax.dot_general(pair[...], up[...], NT, preferred_element_type=f32)
+            all_g[0:BLK, place] = total.reshape(BLK, HEAD).astype(bf16)
+    back = lax.dot_general(all_g[0:BLK, :], up[...], NT, preferred_element_type=f32)
     back_s[...] = back.reshape(SEQ, SPAN, HEAD).astype(bf16)
     step_b = []
     for o, d in enumerate(peers):
@@ -316,74 +346,82 @@
     for i in range(1, GRP):
         total += rp[1 + i]
     prefix[...] = total
-    prefix_low = total.astype(bf16)
-    back_tail = lax.dot_general(prefix_low, up[...], NT, preferred_element_type=f32).astype(bf16)
+    tail = jnp.concatenate([total, jnp.zeros_like(total)], axis=0).astype(bf16)
+    all_g[BLK:DEPTH, :] = tail
+    back_all[BLK:DEPTH, :] = lax.dot_general(tail, up[...], NT, preferred_element_type=f32).astype(bf16)
+    pair[...] = all_g[0:BLK, :]
     for copy in step_j:
         copy.wait_recv()
-    proj_rows = proj_r[...].reshape(BLK, HEAD)
-    proj_tail = proj_tail.astype(f32)
-    prefix_low = prefix_low.astype(f32)
-    for b in range(GRP):
-        cut = slice(b * HEAD, (b + 1) * HEAD)
-        rise = lax.dot_general(proj_rows, pair[:, cut], TN, preferred_element_type=f32)
-        rise += lax.dot_general(proj_tail, prefix_low[:, cut], TN, preferred_element_type=f32)
-        s0[b % 2, b // 2, :, DT:TILE] = rise.astype(bf16)
+    proj_all[0:BLK, :] = proj_r[...].reshape(BLK, HEAD)
+    same = lax.broadcasted_iota(jnp.int32, (HEAD, HEAD), 0) == lax.broadcasted_iota(jnp.int32, (HEAD, HEAD), 1)
+    eye = same.astype(f32).astype(bf16)
+    proj_t[...] = lax.dot_general(eye, proj_all[...], NT, preferred_element_type=f32).astype(bf16)
+    for a in range(NX):
+        cut = slice(a * TILE, (a + 1) * TILE)
+        s0[1, 2, a] = jnp.dot(proj_t[...], all_g[:, cut], preferred_element_type=f32).astype(bf16)
     for copy in step_b:
         copy.wait_recv()
 
-    back_rows = back_r[...].reshape(BLK, HEAD)
-    back_tail = back_tail.astype(f32)
-    for b in range(GRP):
-        cut = slice(b * DT, (b + 1) * DT)
-        part = lax.dot_general(back_rows, own_h[:, cut], TN, preferred_element_type=f32)
-        part += lax.dot_general(back_tail, own_p[:, cut].astype(f32), TN, preferred_element_type=f32)
-        s0[b % 2, b // 2, :, 0:DT] = part.astype(bf16)
+    back_all[0:BLK, :] = back_r[...].reshape(BLK, HEAD)
+    back_t[...] = lax.dot_general(eye, back_all[...], NT, preferred_element_type=f32).astype(bf16)
     sibling = {"grp": grp + 1 - 2 * c}
-    first = remote(s0.at[1 - c], r0, s0_s, s0_r, sibling)
-    first.wait_recv()
-    for i in range(4):
-        s1[i] = (s0[c, i].astype(f32) + r0[i].astype(f32)).astype(bf16)
-    second = []
-    for i in range(1, 4):
-        tz = lax.rem(z + i, 4)
-        second.append(remote(s1.at[tz], r1.at[i - 1], s1_s.at[i], s1_r.at[i], {"grp": tz * 2 + c}))
-    for copy in second:
-        copy.wait_recv()
-    total = s1[z].astype(f32)
-    for i in range(3):
-        total += r1[i].astype(f32)
-    s2[...] = total.reshape(SEQ, SPAN, TILE).astype(bf16)
-    third = []
-    for o, d in enumerate(peers):
-        third.append(remote(s2.at[d], r2.at[o], s2_s.at[o], s2_r.at[o], {"seq": d}))
-    for copy in third:
-        copy.wait_recv()
-    total = s2[me].astype(f32)
-    for o in range(SEQ - 1):
-        total += r2[o].astype(f32)
-    fin[...] = total.astype(bf16)
-    fourth = []
-    for o, d in enumerate(peers):
-        fourth.append(remote(fin, a2.at[me], a2_s.at[o], a2_r.at[o], {"seq": d}))
-    a2[me] = fin[...]
-    for copy in fourth:
-        copy.wait_recv()
-    fifth = []
-    for i in range(1, 4):
-        tz = lax.rem(z + i, 4)
-        fifth.append(remote(a2, out.at[c, z], a1_s.at[i], a1_r.at[i], {"grp": tz * 2 + c}))
-    out[c, z] = a2[...]
+    zero, first, second, third, fourth, fifth = [], [], [], [], [], []
+    for t in range(TYPES):
+        for half in range(2):
+            for a in range(NX):
+                n = (half * TYPES + t) * NX + a
+                if n < D // TILE:
+                    cut = slice(n * TILE, (n + 1) * TILE)
+                    part = jnp.dot(back_t[...], own_h[:, cut], preferred_element_type=f32)
+                    s0[half, t, a] = part.astype(bf16)
+        zero.append(remote(s0.at[1 - c, t], r0.at[t], s0_s.at[t], s0_r.at[t], sibling))
+    for t in range(TYPES):
+        zero[t].wait_recv()
+        for a in range(NX):
+            s1[t, a] = (s0[c, t, a].astype(f32) + r0[t, a].astype(f32)).astype(bf16)
+        for i in range(1, NX):
+            there = lax.rem(on_line[t] + i, NX)
+            first.append(remote(s1.at[t, there], r1.at[t, i - 1], s1_s.at[t, i], s1_r.at[t, i], line(t, i)))
+    for t in range(TYPES):
+        for copy in first[t * 3 : t * 3 + 3]:
+            copy.wait_recv()
+        total = s1[t, on_line[t]].astype(f32)
+        for i in range(NX - 1):
+            total += r1[t, i].astype(f32)
+        s2[t] = total.reshape(SEQ, SPAN, TILE).astype(bf16)
+        for o in range(SEQ - 1):
+            e = lax.rem(on_plane[t] + o + 1, SEQ)
+            second.append(remote(s2.at[t, e], r2.at[t, o], s2_s.at[t, o], s2_r.at[t, o], plane(t, e)))
+    for t in range(TYPES):
+        for copy in second[t * 15 : t * 15 + 15]:
+            copy.wait_recv()
+        total = s2[t, on_plane[t]].astype(f32)
+        for o in range(SEQ - 1):
+            total += r2[t, o].astype(f32)
+        out[c, t, on_line[t], on_plane[t]] = total.astype(bf16)
+        piece = out.at[c, t, on_line[t], on_plane[t]]
+        for o in range(SEQ - 1):
+            e = lax.rem(on_plane[t] + o + 1, SEQ)
+            third.append(remote(piece, piece, a2_s.at[t, o], a2_r.at[t, o], plane(t, e)))
+    for t in range(TYPES):
+        for copy in third[t * 15 : t * 15 + 15]:
+            copy.wait_recv()
+        piece = out.at[c, t, on_line[t]]
+        for i in range(1, NX):
+            fourth.append(remote(piece, piece, a1_s.at[t, i], a1_r.at[t, i], line(t, i)))
+    for t in range(TYPES):
+        for copy in fourth[t * 3 : t * 3 + 3]:
+            copy.wait_recv()
+        fifth.append(remote(out.at[c, t], out.at[c, t], a0_s.at[t], a0_r.at[t], sibling))
     for copy in fifth:
         copy.wait_recv()
-    sixth = remote(out.at[c], out.at[c], a0_s, a0_r, sibling)
-    sixth.wait_recv()
 
     for pairs in step_x:
         for copy in pairs:
             copy.wait_send()
     for copy in (
         step_q + step_y + step_j + step_e + step_t + step_p + step_b
-        + [first] + second + third + fourth + fifth + [sixth]
+        + zero + first + second + third + fourth + fifth
     ):
         copy.wait_send()
 
@@ -402,28 +440,30 @@
         out_shape=(
             jax.ShapeDtypeStruct((BLK, 2 * KVW), bf16),
             jax.ShapeDtypeStruct((SPAN, 2 * KVW), f32),
-            jax.ShapeDtypeStruct((2, 4, SEQ, SPAN, TILE), bf16),
+            jax.ShapeDtypeStruct((2, TYPES, NX, SEQ, SPAN, TILE), bf16),
         ),
         in_specs=[smem()] * 2 + [hbm()] * 11 + [vmem()] * 2,
         out_specs=(vmem(),) * 3,
         scratch_shapes=[
             low(NX, BLK, DT), low(NX, BLK, DT), wide(NX, 8, W), low(TREE + 2 * BLK, PAIR),
-            low(BLK, 4 * DT), low(BLK, 4 * DT), low(BLK, D), low(SPAN, D), low(HEAD, D),
+            low(BLK, 4 * DT), low(BLK, 4 * DT), low(DEPTH, D), low(SPAN, D), low(HEAD, D),
             low(GRP, BLK, PAIR), low(HEAD, 2 * KVW), wide(KV, 8, W),
+            low(DEPTH, 2 * KVW), low(DEPTH, HEAD), low(HEAD, DEPTH), low(DEPTH, HEAD), low(HEAD, DEPTH),
             wide(TREE + 2 * BLK, W), wide(TREE + 2 * BLK, PAIR), low(W, HEAD), low(W, HEAD),
             low(GROUP, W), low(GROUP, W), wide(8, W), wide(8, W), wide(GROUP, BLK),
             low(SEQ, SEQ + 2, SPAN, PAIR), low(SEQ, SEQ + 2, SPAN, PAIR),
             low(SEQ, SPAN, HEAD), low(SEQ, SPAN, HEAD),
             wide(GRP, SPAN, 2 * KVW), wide(GRP + 1, SPAN, 2 * KVW),
             low(SEQ, SPAN, HEAD), low(SEQ, SPAN, HEAD),
-            low(2, 4, BLK, TILE), low(4, BLK, TILE), low(4, BLK, TILE), low(3, BLK, TILE),
-            low(SEQ, SPAN, TILE), low(SEQ, SPAN, TILE), low(SPAN, TILE), low(SEQ, SPAN, TILE),
+            low(2, TYPES, NX, BLK, TILE), low(TYPES, NX, BLK, TILE), low(TYPES, NX, BLK, TILE),
+            low(TYPES, NX - 1, BLK, TILE), low(TYPES, SEQ, SPAN, TILE), low(TYPES, SEQ - 1, SPAN, TILE),
             dma((12,)),
             dma((2, NX)), dma((2, NX)), dma((NX, NX)), dma((NX, NX)), dma((3, NX)), dma((3, NX)),
             dma((5, SEQ)), dma((5, SEQ)), dma((SEQ,)), dma((SEQ,)), dma((SEQ,)), dma((SEQ,)),
             dma((GRP,)), dma((GRP,)),
-            dma, dma, dma((4,)), dma((4,)), dma((SEQ,)), dma((SEQ,)), dma((SEQ,)), dma((SEQ,)),
-            dma((4,)), dma((4,)), dma, dma,
+            dma((TYPES,)), dma((TYPES,)), dma((TYPES, NX)), dma((TYPES, NX)),
+            dma((TYPES, SEQ)), dma((TYPES, SEQ)), dma((TYPES, SEQ)), dma((TYPES, SEQ)),
+            dma((TYPES, NX)), dma((TYPES, NX)), dma((TYPES,)), dma((TYPES,)),
         ],
         compiler_params=pltpu.CompilerParams(
             collective_id=0, has_side_effects=True, vmem_limit_bytes=56 * 2**20
@@ -434,27 +474,37 @@
 
 def spread_kernel(summed, down, rise):
     factor = 2.0 / (GRP * SEQ)
-    b = pl.program_id(0)
-    part = summed[0, 0].reshape(BLK, TILE).astype(f32) * factor
-    down[...] = part[:, 0:DT]
-    rise[0] = jnp.where(b < 4, part[0:64, DT:TILE], part[64:128, DT:TILE])
+    step = pl.program_id(0)
+
+    @pl.when(step < 5)
+    def _():
+        for a in range(NX):
+            part = summed[0, a].reshape(BLK, TILE).astype(f32)
+            down[:, a * TILE : (a + 1) * TILE] = part * factor
+
+    @pl.when(step == 5)
+    def _():
+        for a in range(NX):
+            part = summed[0, a].reshape(BLK, TILE).astype(f32)
+            side = a // 2
+            rise[side, :, (a % 2) * TILE : (a % 2 + 1) * TILE] = part[side * 64 : side * 64 + 64] * factor
 
 
 def spread(summed):
     return pl.pallas_call(
         spread_kernel,
-        grid=(GRP,),
+        grid=(2 * TYPES,),
         out_shape=(
             jax.ShapeDtypeStruct((BLK, D), f32),
             jax.ShapeDtypeStruct((2, 64, KVW), f32),
         ),
-        in_specs=[pl.BlockSpec((1, 1, SEQ, SPAN, TILE), lambda b: (b % 2, b // 2, 0, 0, 0))],
+        in_specs=[pl.BlockSpec((1, NX, SEQ, SPAN, TILE), lambda b: (b, 0, 0, 0, 0))],
         out_specs=(
-            pl.BlockSpec((BLK, DT), lambda b: (0, b)),
-            pl.BlockSpec((1, 64, HEAD), lambda b: (b // 4, 0, b % 4)),
+            pl.BlockSpec((BLK, NX * TILE), lambda b: (0, jnp.minimum(b, 4))),
+            pl.BlockSpec((2, 64, KVW), lambda b: (0, 0, 0)),
         ),
         name="spread",
-    )(summed)
+    )(summed.reshape(2 * TYPES, NX, SEQ, SPAN, TILE))
 
 
 def on_device(

time: 110 us -> 98.8 us (0.90)
  Pallas kernels: 107 us -> 96.6 us
    pallas_call x1, Pallas kernels: 102 us -> 91.6 us  [backward(): pl.pallas_call(kernel, out_shape=(jax.ShapeDtypeStruct((BLK, 2 * KVW), bf...]
where the time goes in v3:
time: 98.8 us; the launch traced here: 98.6 us
  Pallas kernels  96.6 us (98%)
  local copies, waits for them, and re-layouts  1.33 us (1%)
    pallas_call x1, Pallas kernels, backward(): pl.pallas_call(kernel, out_shape=(jax.ShapeDtypeStruct((BLK, 2 * KVW), bf...  91.6 us
    pallas_call x1, Pallas kernels, spread(): pl.pallas_call(spread_kernel, grid=(2 * TYPES,), out_shape=(jax.ShapeDtyp...  4.92 us

profile of v3, /device:TPU:1, one launch (start us, length us, event | category | flops | bytes accessed | tf_op | source)
XLA Modules:
  0.0 98.6 jit_solution(9181622267963647347)
XLA Ops:
  0.6 91.6 %backward.1 = (bf16[128,1024]{1,0:T(8,128)(2,1)}, f32[8,1024]{1,0:T(8,128)}, bf16[2,3,4,16,8,256]{5,4,3,2,1,0:T(8,128)(2,1)}) custom-call(s32[16,16]{1,0:T(8,128)} %bitcast.28, s32[1,2]{1,0:T(1,128)} %listed.1, bf16[128,2560]{1,0:T(8,128)(2,1)} %bitcast.18, bf16[128,2560]{1,0:T(8,128)(2,1)} %bitcast.19, bf16[128,2560]{1,0:T(8,128)(2,1)} %bitcast.20, ...), custom_call_target="tpu_custom_call" | custom-call | tf_op jit(solution)/shard_map/backward/pallas_call | solution.py:438
  92.3 0.0 copy-start
  92.3 0.0 copy-start.1
  92.3 4.9 %spread.1 = (f32[128,5120]{1,0:T(8,128)}, f32[2,64,512]{2,1,0:T(8,128)}) custom-call(bf16[6,4,16,8,256]{4,3,2,1,0:T(8,128)(2,1)} %bitcast.16), custom_call_target="tpu_custom_call" | custom-call | tf_op jit(solution)/shard_map/spread/pallas_call | solution.py:494
  97.2 0.0 copy-done
  97.2 0.7 copy.21
  97.9 0.0 copy-done.1
  97.9 0.6 copy.22
Async XLA Ops:
  92.3 4.9 %copy-start = (bf16[128,1024]{1,0:T(8,128)(2,1)S(1)}, bf16[128,1024]{1,0:T(8,128)(2,1)}, u32[]{:S(2)}) copy-start(bf16[128,1024]{1,0:T(8,128)(2,1)} %get-tuple-element.9) | copy-start | bytes 786436
  92.3 5.6 %copy-start.1 = (f32[8,1024]{1,0:T(8,128)S(1)}, f32[8,1024]{1,0:T(8,128)}, u32[]{:S(2)}) copy-start(f32[8,1024]{1,0:T(8,128)} %get-tuple-element.10) | copy-start | bytes 98308

commit v4 on v3

--- a/solution.py
+++ b/solution.py
@@ -76,9 +76,9 @@
     mask, listed, q, g, saved, k, v, hidden, hidden_p, pool_k, pool_v, down_k, down_v, up_k, up_v,
     pair, prefix, out,
     q_in, g_in, delta_in, kv, own_g, own_s, own_h, own_p, down, pool, up, delta_out, all_g, back_all, back_t, proj_all, proj_t,
-    s_ref, acc, qs, gs, pb, dsb, top, low, diag,
+    s_ref, acc, qs, gs, pb, dsb, stat, diag,
     tsend, rt, proj_s, proj_r, pt, rp, back_s, back_r,
-    s0, r0, s1, r1, s2, r2,
+    s0, r0, s1, r1, s2, r2, full, own_x,
     sem_in, kvx_s, kvx_r, kvy_s, kvy_r, q_s, q_r, t_s, t_r, j_s, j_r, b_s, b_r, p_s, p_r,
     s0_s, s0_r, s1_s, s1_r, s2_s, s2_r, a2_s, a2_r, a1_s, a1_r, a0_s, a0_r,
 ):
@@ -141,41 +141,54 @@
     delta_in[x] = delta_out[x]
     greeted(met)
 
-    step_x = []
+    step_x, step_y, step_q, step_g = ([], []), ([], []), [], []
+
+    def send_x(n, source, lanes):
+        for i in range(1, NX):
+            tx = lax.rem(x + i, NX)
+            step_x[n].append(
+                remote(
+                    source.at[:, cols(tx, HEAD)], kv.at[mine, lanes], kvx_s.at[n, i], kvx_r.at[n, i],
+                    {"seq": tx * NX + y},
+                )
+            )
+
+    def send_y(n, k, lanes):
+        block = rows(lax.rem(x + NX - k, NX) * NX + y, BLK)
+        for i in range(1, NX):
+            device = {"seq": x * NX + lax.rem(y + i, NX)}
+            piece = kv.at[block, lanes]
+            step_y[n].append(remote(piece, piece, kvy_s.at[n, k, i], kvy_r.at[n, k, i], device))
+
+    def send_rows(n, source, target, steps):
+        for i in range(1, NX):
+            tx = lax.rem(x + i, NX)
+            steps.append(
+                remote(
+                    source.at[:, cols(tx, DT)], target.at[x], q_s.at[n, i], q_r.at[n, i],
+                    {"seq": tx * NX + y},
+                )
+            )
+
+    key_lanes, value_lanes = slice(0, HEAD), slice(HEAD, PAIR)
+    send_x(0, k, key_lanes)
+    keep[0].wait()
+    send_y(0, 0, key_lanes)
+    send_rows(0, q, q_in, step_q)
+    for n in (1, 3, 2):
+        step_x[0][n - 1].wait_recv()
+        send_y(0, n, key_lanes)
+    send_x(1, v, value_lanes)
+    keep[1].wait()
+    send_y(1, 0, value_lanes)
     for i in range(1, NX):
         tx = lax.rem(x + i, NX)
         device = {"seq": tx * NX + y}
-        step_x.append(
-            (
-                remote(k.at[:, cols(tx, HEAD)], kv.at[mine, 0:HEAD], kvx_s.at[0, i], kvx_r.at[0, i], device),
-                remote(v.at[:, cols(tx, HEAD)], kv.at[mine, HEAD:PAIR], kvx_s.at[1, i], kvx_r.at[1, i], device),
-            )
-        )
-    keep[0].wait()
-    keep[1].wait()
-    step_y = []
-
-    def forward(n):
-        block = rows(lax.rem(x + NX - n, NX) * NX + y, BLK)
-        for i in range(1, NX):
-            device = {"seq": x * NX + lax.rem(y + i, NX)}
-            step_y.append(remote(kv.at[block], kv.at[block], kvy_s.at[n, i], kvy_r.at[n, i], device))
-
-    forward(0)
-    step_q = []
-    for i in range(1, NX):
-        tx = lax.rem(x + i, NX)
-        device = {"seq": tx * NX + y}
-        step_q.append(remote(delta_out.at[tx], delta_in.at[x], q_s.at[2, i], q_r.at[2, i], device))
-    for i in range(1, NX):
-        tx = lax.rem(x + i, NX)
-        device = {"seq": tx * NX + y}
-        step_q.append(remote(q.at[:, cols(tx, DT)], q_in.at[x], q_s.at[0, i], q_r.at[0, i], device))
-        step_q.append(remote(g.at[:, cols(tx, DT)], g_in.at[x], q_s.at[1, i], q_r.at[1, i], device))
+        step_g.append(remote(delta_out.at[tx], delta_in.at[x], q_s.at[2, i], q_r.at[2, i], device))
+    send_rows(1, g, g_in, step_g)
     for n in (1, 3, 2):
-        for copy in step_x[n - 1]:
-            copy.wait_recv()
-        forward(n)
+        step_x[1][n - 1].wait_recv()
+        send_y(1, n, value_lanes)
 
     for i in range(6, 10):
         keep[i].wait()
@@ -201,31 +214,43 @@
     query_at = lax.broadcasted_iota(jnp.int32, (GROUP, BLK), 1)
     diag[...] = jnp.where(key_at <= y * BLK + query_at, 0.0, MASKED).astype(f32)
     keep[2].wait()
-    keep[3].wait()
-    for copy in step_q + step_y:
-        copy.wait_recv()
-
-    def rollout(step, carry):
+    for copy in step_q + step_y[0]:
+        copy.wait_recv()
+
+    def score_rows(kk):
+        return 2 * BLK * kk * (kk + 2)
+
+    def score_place(start, m):
+        return pl.ds(pl.multiple_of(start + 2 * BLK + m * GROUP, 2 * BLK), GROUP)
+
+    def ends_place(start):
+        return pl.ds(pl.multiple_of(start, 2 * BLK), 2 * BLK)
+
+    ends = slice(TREE, TREE + 2 * BLK)
+
+    def scores(step, carry):
         kk = NX - 1 - step
         r = y + NX * kk
+        start = score_rows(kk)
         for t in range(REP):
             span = slice(t * BLK, (t + 1) * BLK)
-            qs[span, :] = q_in[kk, :, span]
-            gs[span, :] = g_in[kk, :, span]
+            qs[kk, span, :] = q_in[kk, :, span]
+        top = stat.at[0, kk]
+        low = stat.at[1, kk]
         top[...] = jnp.full_like(top, MASKED)
         low[...] = jnp.zeros_like(low)
 
         def hides(m):
             return [(mask[r, m * 4 + b].astype(f32) - 1.0) * 1e30 for b in range(4)]
 
-        def score(place, hidden_by, diagonal, n):
+        def score(place, into, hidden_by, diagonal, n):
             for lo, hi in CHUNKS:
                 w = hi - lo
-                s = lax.dot_general(kv[place, 0:HEAD], qs[lo:hi, :], NT, preferred_element_type=f32)
+                s = lax.dot_general(kv[place, 0:HEAD], qs[kk, lo:hi, :], NT, preferred_element_type=f32)
                 s = s * (SCALE * LOG2E)
                 if diagonal:
                     s = s + jnp.concatenate([diag[...]] * (w // BLK), axis=1)
-                s_ref[place, lo:hi] = s
+                s_ref[into, lo:hi] = s
                 cut = s.reshape(n, BLK // 8, 8, w)
                 before = top[:, lo:hi]
                 now = before
@@ -238,38 +263,55 @@
                 top[:, lo:hi] = now
 
         def score_group(m, cc):
-            score(rows(m, GROUP), hides(m), False, 4)
+            score(rows(m, GROUP), score_place(start, m), hides(m), False, 4)
             return cc
 
-        ends = slice(TREE, TREE + 2 * BLK)
-        score(ends, [0.0, 0.0], False, 2)
+        score(ends, ends_place(start), [0.0, 0.0], False, 2)
         lax.fori_loop(0, kk, score_group, 0)
-        score(rows(kk, GROUP), hides(kk), True, 4)
+        score(rows(kk, GROUP), score_place(start, kk), hides(kk), True, 4)
         best = jnp.max(top[...], axis=0, keepdims=True)
         total = jnp.sum(low[...] * jnp.exp2(top[...] - best), axis=0, keepdims=True)
         top[...] = jnp.broadcast_to(best + jnp.log2(total), (8, W))
-        low[...] = delta_in[kk]
-
-        def grads(place, hidden_by, n):
+        return carry
+
+    lax.fori_loop(0, NX, scores, 0)
+    keep[3].wait()
+    for copy in step_g + step_y[1]:
+        copy.wait_recv()
+
+    def rollout(step, carry):
+        kk = NX - 1 - step
+        r = y + NX * kk
+        start = score_rows(kk)
+        for t in range(REP):
+            span = slice(t * BLK, (t + 1) * BLK)
+            gs[span, :] = g_in[kk, :, span]
+        top = stat.at[0, kk]
+        low = delta_in.at[kk]
+
+        def hides(m):
+            return [(mask[r, m * 4 + b].astype(f32) - 1.0) * 1e30 for b in range(4)]
+
+        def grads(place, into, hidden_by, n):
             for lo, hi in CHUNKS:
                 w = hi - lo
                 dp = lax.dot_general(kv[place, HEAD:PAIR], gs[lo:hi, :], NT, preferred_element_type=f32)
                 dp = dp.reshape(n, BLK // 8, 8, w)
-                cut = s_ref[place, lo:hi].reshape(n, BLK // 8, 8, w)
+                cut = s_ref[into, lo:hi].reshape(n, BLK // 8, 8, w)
                 for b in range(n):
                     span = slice(b * BLK, (b + 1) * BLK)
                     p = jnp.exp2(cut[b] - (top[:, lo:hi] - hidden_by[b])[None])
                     ds = p * (dp[b] - low[:, lo:hi][None])
                     pb[span, lo:hi] = p.reshape(BLK, w).astype(bf16)
                     dsb[span, lo:hi] = ds.reshape(BLK, w).astype(bf16)
-            acc[place, 0:HEAD] += jnp.dot(dsb[0 : n * BLK, :], qs[...], preferred_element_type=f32)
+            acc[place, 0:HEAD] += jnp.dot(dsb[0 : n * BLK, :], qs[kk], preferred_element_type=f32)
             acc[place, HEAD:PAIR] += jnp.dot(pb[0 : n * BLK, :], gs[...], preferred_element_type=f32)
 
         def grads_group(m, cc):
-            grads(rows(m, GROUP), hides(m), 4)
+            grads(rows(m, GROUP), score_place(start, m), hides(m), 4)
             return cc
 
-        grads(ends, [0.0, 0.0], 2)
+        grads(ends, ends_place(start), [0.0, 0.0], 2)
         lax.fori_loop(0, kk + 1, grads_group, 0)
 
         for b in range(4):
@@ -345,11 +387,12 @@
     total = pt[grp]
     for i in range(1, GRP):
         total += rp[1 + i]
-    prefix[...] = total
+    own_x[...] = total
+    keep.append(local(own_x, prefix, 12))
     tail = jnp.concatenate([total, jnp.zeros_like(total)], axis=0).astype(bf16)
     all_g[BLK:DEPTH, :] = tail
     back_all[BLK:DEPTH, :] = lax.dot_general(tail, up[...], NT, preferred_element_type=f32).astype(bf16)
-    pair[...] = all_g[0:BLK, :]
+    keep.append(local(all_g.at[0:BLK], pair, 13))
     for copy in step_j:
         copy.wait_recv()
     proj_all[0:BLK, :] = proj_r[...].reshape(BLK, HEAD)
@@ -398,29 +441,29 @@
         total = s2[t, on_plane[t]].astype(f32)
         for o in range(SEQ - 1):
             total += r2[t, o].astype(f32)
-        out[c, t, on_line[t], on_plane[t]] = total.astype(bf16)
-        piece = out.at[c, t, on_line[t], on_plane[t]]
+        full[t, on_line[t], on_plane[t]] = total.astype(bf16)
+        piece = full.at[t, on_line[t], on_plane[t]]
         for o in range(SEQ - 1):
             e = lax.rem(on_plane[t] + o + 1, SEQ)
             third.append(remote(piece, piece, a2_s.at[t, o], a2_r.at[t, o], plane(t, e)))
     for t in range(TYPES):
         for copy in third[t * 15 : t * 15 + 15]:
             copy.wait_recv()
-        piece = out.at[c, t, on_line[t]]
+        piece = full.at[t, on_line[t]]
         for i in range(1, NX):
             fourth.append(remote(piece, piece, a1_s.at[t, i], a1_r.at[t, i], line(t, i)))
     for t in range(TYPES):
         for copy in fourth[t * 3 : t * 3 + 3]:
             copy.wait_recv()
-        fifth.append(remote(out.at[c, t], out.at[c, t], a0_s.at[t], a0_r.at[t], sibling))
+        fifth.append(remote(full.at[t], out.at[c, t], a0_s.at[t], a0_r.at[t], sibling))
+        keep.append(local(full.at[t], out.at[c, t], 14 + t))
     for copy in fifth:
         copy.wait_recv()
-
-    for pairs in step_x:
-        for copy in pairs:
-            copy.wait_send()
+    for copy in keep[12:]:
+        copy.wait()
+
     for copy in (
-        step_q + step_y + step_j + step_e + step_t + step_p + step_b
+        step_x[0] + step_x[1] + step_y[0] + step_y[1] + step_q + step_g + step_j + step_e + step_t + step_p + step_b
         + zero + first + second + third + fourth + fifth
     ):
         copy.wait_send()
@@ -443,22 +486,23 @@
             jax.ShapeDtypeStruct((2, TYPES, NX, SEQ, SPAN, TILE), bf16),
         ),
         in_specs=[smem()] * 2 + [hbm()] * 11 + [vmem()] * 2,
-        out_specs=(vmem(),) * 3,
+        out_specs=(hbm(),) * 3,
         scratch_shapes=[
             low(NX, BLK, DT), low(NX, BLK, DT), wide(NX, 8, W), low(TREE + 2 * BLK, PAIR),
             low(BLK, 4 * DT), low(BLK, 4 * DT), low(DEPTH, D), low(SPAN, D), low(HEAD, D),
             low(GRP, BLK, PAIR), low(HEAD, 2 * KVW), wide(KV, 8, W),
             low(DEPTH, 2 * KVW), low(DEPTH, HEAD), low(HEAD, DEPTH), low(DEPTH, HEAD), low(HEAD, DEPTH),
-            wide(TREE + 2 * BLK, W), wide(TREE + 2 * BLK, PAIR), low(W, HEAD), low(W, HEAD),
-            low(GROUP, W), low(GROUP, W), wide(8, W), wide(8, W), wide(GROUP, BLK),
+            wide(2 * BLK * NX * (NX + 2), W), wide(TREE + 2 * BLK, PAIR), low(NX, W, HEAD), low(W, HEAD),
+            low(GROUP, W), low(GROUP, W), wide(2, NX, 8, W), wide(GROUP, BLK),
             low(SEQ, SEQ + 2, SPAN, PAIR), low(SEQ, SEQ + 2, SPAN, PAIR),
             low(SEQ, SPAN, HEAD), low(SEQ, SPAN, HEAD),
             wide(GRP, SPAN, 2 * KVW), wide(GRP + 1, SPAN, 2 * KVW),
             low(SEQ, SPAN, HEAD), low(SEQ, SPAN, HEAD),
             low(2, TYPES, NX, BLK, TILE), low(TYPES, NX, BLK, TILE), low(TYPES, NX, BLK, TILE),
             low(TYPES, NX - 1, BLK, TILE), low(TYPES, SEQ, SPAN, TILE), low(TYPES, SEQ - 1, SPAN, TILE),
-            dma((12,)),
-            dma((2, NX)), dma((2, NX)), dma((NX, NX)), dma((NX, NX)), dma((3, NX)), dma((3, NX)),
+            low(TYPES, NX, SEQ, SPAN, TILE), wide(SPAN, 2 * KVW),
+            dma((17,)),
+            dma((2, NX)), dma((2, NX)), dma((2, NX, NX)), dma((2, NX, NX)), dma((3, NX)), dma((3, NX)),
             dma((5, SEQ)), dma((5, SEQ)), dma((SEQ,)), dma((SEQ,)), dma((SEQ,)), dma((SEQ,)),
             dma((GRP,)), dma((GRP,)),
             dma((TYPES,)), dma((TYPES,)), dma((TYPES, NX)), dma((TYPES, NX)),
@@ -472,7 +516,7 @@
     )(*operands)
 
 
-def spread_kernel(summed, down, rise):
+def spread_kernel(summed, pair, prefix, down, rise, pair_out, prefix_out):
     factor = 2.0 / (GRP * SEQ)
     step = pl.program_id(0)
 
@@ -481,6 +525,11 @@
         for a in range(NX):
             part = summed[0, a].reshape(BLK, TILE).astype(f32)
             down[:, a * TILE : (a + 1) * TILE] = part * factor
+
+    @pl.when(step == 0)
+    def _():
+        pair_out[...] = pair[...]
+        prefix_out[...] = prefix[...]
 
     @pl.when(step == 5)
     def _():
@@ -490,21 +539,29 @@
             rise[side, :, (a % 2) * TILE : (a % 2 + 1) * TILE] = part[side * 64 : side * 64 + 64] * factor
 
 
-def spread(summed):
+def spread(summed, pair, prefix):
     return pl.pallas_call(
         spread_kernel,
         grid=(2 * TYPES,),
         out_shape=(
             jax.ShapeDtypeStruct((BLK, D), f32),
             jax.ShapeDtypeStruct((2, 64, KVW), f32),
+            jax.ShapeDtypeStruct((BLK, 2 * KVW), bf16),
+            jax.ShapeDtypeStruct((SPAN, 2 * KVW), f32),
         ),
-        in_specs=[pl.BlockSpec((1, NX, SEQ, SPAN, TILE), lambda b: (b, 0, 0, 0, 0))],
+        in_specs=[
+            pl.BlockSpec((1, NX, SEQ, SPAN, TILE), lambda b: (b, 0, 0, 0, 0)),
+            pl.BlockSpec((BLK, 2 * KVW), lambda b: (0, 0)),
+            pl.BlockSpec((SPAN, 2 * KVW), lambda b: (0, 0)),
+        ],
         out_specs=(
             pl.BlockSpec((BLK, NX * TILE), lambda b: (0, jnp.minimum(b, 4))),
             pl.BlockSpec((2, 64, KVW), lambda b: (0, 0, 0)),
+            pl.BlockSpec((BLK, 2 * KVW), lambda b: (0, 0)),
+            pl.BlockSpec((SPAN, 2 * KVW), lambda b: (0, 0)),
         ),
         name="spread",
-    )(summed.reshape(2 * TYPES, NX, SEQ, SPAN, TILE))
+    )(summed.reshape(2 * TYPES, NX, SEQ, SPAN, TILE), pair, prefix)
 
 
 def on_device(
@@ -516,7 +573,7 @@
         key_rows[0, 0], value_rows[0, 0], hidden_rows[0, 0], prefix_hidden[0],
         prefix_keys, prefix_values, key_down.T, value_down.T, key_up, value_up,
     )
-    down, rise = spread(summed)
+    down, rise, pair, prefix = spread(summed, pair, prefix)
     down = jnp.swapaxes(down.reshape(2, BLK // 2, D), 1, 2)
     return pair[None], prefix[None], down, rise
 

time: 98.8 us -> 92.2 us (0.933)
  Pallas kernels: 96.6 us -> 91.3 us
  local copies, waits for them, and re-layouts: 1.33 us -> 0 us
    pallas_call x1, Pallas kernels: 91.6 us -> 86.2 us  [backward(): pl.pallas_call(kernel, out_shape=(jax.ShapeDtypeStruct((BLK, 2 * KVW), bf...]
    unnamed x6 -> x0, local copies, waits for them, and re-layouts: 1.33 us -> none
where the time goes in v4:
time: 92.2 us; the launch traced here: 92 us
  Pallas kernels  91.3 us (99%)
    pallas_call x1, Pallas kernels, backward(): pl.pallas_call(kernel, out_shape=(jax.ShapeDtypeStruct((BLK, 2 * KVW), bf...  86.2 us
    pallas_call x1, Pallas kernels, spread(): pl.pallas_call(spread_kernel, grid=(2 * TYPES,), out_shape=(jax.ShapeDtyp...  5.09 us

profile of v4, /device:TPU:1, one launch (start us, length us, event | category | flops | bytes accessed | tf_op | source)
XLA Modules:
  0.0 92.0 jit_solution(15260315898567785625)
XLA Ops:
  0.6 86.2 %backward.1 = (bf16[128,1024]{1,0:T(8,128)(2,1)}, f32[8,1024]{1,0:T(8,128)}, bf16[2,3,4,16,8,256]{5,4,3,2,1,0:T(8,128)(2,1)}) custom-call(s32[16,16]{1,0:T(8,128)} %bitcast.26, s32[1,2]{1,0:T(1,128)} %listed.1, bf16[128,2560]{1,0:T(8,128)(2,1)} %bitcast.18, bf16[128,2560]{1,0:T(8,128)(2,1)} %bitcast.19, bf16[128,2560]{1,0:T(8,128)(2,1)} %bitcast.20, ...), custom_call_target="tpu_custom_call" | custom-call | tf_op jit(solution)/shard_map/backward/pallas_call | solution.py:481
  86.9 5.1 %spread.1 = (f32[128,5120]{1,0:T(8,128)}, f32[2,64,512]{2,1,0:T(8,128)}, bf16[128,1024]{1,0:T(8,128)(2,1)}, f32[8,1024]{1,0:T(8,128)}) custom-call(bf16[6,4,16,8,256]{4,3,2,1,0:T(8,128)(2,1)} %bitcast.16, bf16[128,1024]{1,0:T(8,128)(2,1)} %get-tuple-element.12.pair, f32[8,1024]{1,0:T(8,128)} %get-tuple-element.13.prefix), custom_call_target="tpu_custom_call" | custom-call | tf_op jit(solution)/shard_map/spread/pallas_call | solution.py:543

commit v5 on v4

--- a/solution.py
+++ b/solution.py
@@ -172,23 +172,21 @@
 
     key_lanes, value_lanes = slice(0, HEAD), slice(HEAD, PAIR)
     send_x(0, k, key_lanes)
+    send_x(1, v, value_lanes)
     keep[0].wait()
     send_y(0, 0, key_lanes)
-    send_rows(0, q, q_in, step_q)
-    for n in (1, 3, 2):
-        step_x[0][n - 1].wait_recv()
-        send_y(0, n, key_lanes)
-    send_x(1, v, value_lanes)
     keep[1].wait()
     send_y(1, 0, value_lanes)
+    send_rows(0, q, q_in, step_q)
     for i in range(1, NX):
         tx = lax.rem(x + i, NX)
         device = {"seq": tx * NX + y}
         step_g.append(remote(delta_out.at[tx], delta_in.at[x], q_s.at[2, i], q_r.at[2, i], device))
     send_rows(1, g, g_in, step_g)
-    for n in (1, 3, 2):
-        step_x[1][n - 1].wait_recv()
-        send_y(1, n, value_lanes)
+    for side, lanes in ((0, key_lanes), (1, value_lanes)):
+        for n in (1, 3, 2):
+            step_x[side][n - 1].wait_recv()
+            send_y(side, n, lanes)
 
     for i in range(6, 10):
         keep[i].wait()
@@ -279,6 +277,13 @@
     for copy in step_g + step_y[1]:
         copy.wait_recv()
 
+    def term(n, first_block, count, o):
+        part = pl.ds(first_block, count)
+        return pltpu.make_async_remote_copy(
+            src_ref=tsend.at[peers[o], part], dst_ref=rt.at[me, part], send_sem=t_s.at[n, o],
+            recv_sem=t_r.at[n, o], device_id={"seq": peers[o]}, device_id_type=MESH,
+        )
+
     def rollout(step, carry):
         kk = NX - 1 - step
         r = y + NX * kk
@@ -312,42 +317,30 @@
             return cc
 
         grads(ends, ends_place(start), [0.0, 0.0], 2)
-        lax.fori_loop(0, kk + 1, grads_group, 0)
-
+
+        @pl.when(step == NX - 1)
+        def _():
+            for i in range(2):
+                part = acc[TREE + i * BLK : TREE + (i + 1) * BLK, :].reshape(SEQ, SPAN, PAIR)
+                tsend[:, SEQ + i, :, 0:HEAD] = (part[:, :, 0:HEAD] * SCALE).astype(bf16)
+                tsend[:, SEQ + i, :, HEAD:PAIR] = part[:, :, HEAD:PAIR].astype(bf16)
+            for o in range(SEQ - 1):
+                term(4, SEQ, 2, o).start()
+
+        grads_group(kk, 0)
         for b in range(4):
             j = kk * 4 + b
             part = acc[rows(j, BLK), :].reshape(SEQ, SPAN, PAIR)
             tsend[:, j, :, 0:HEAD] = (part[:, :, 0:HEAD] * SCALE).astype(bf16)
             tsend[:, j, :, HEAD:PAIR] = part[:, :, HEAD:PAIR].astype(bf16)
-
-        @pl.when(step < NX - 1)
-        def _():
-            for o, d in enumerate(peers):
-                four = pl.ds(kk * 4, 4)
-                remote(tsend.at[d, four], rt.at[me, four], t_s.at[kk, o], t_r.at[kk, o], {"seq": d})
-
+        for o in range(SEQ - 1):
+            term(kk, kk * 4, 4, o).start()
+        lax.fori_loop(0, kk, grads_group, 0)
         return carry
 
     lax.fori_loop(0, NX, rollout, 0)
-    for i in range(2):
-        part = acc[TREE + i * BLK : TREE + (i + 1) * BLK, :].reshape(SEQ, SPAN, PAIR)
-        tsend[:, SEQ + i, :, 0:HEAD] = (part[:, :, 0:HEAD] * SCALE).astype(bf16)
-        tsend[:, SEQ + i, :, HEAD:PAIR] = part[:, :, HEAD:PAIR].astype(bf16)
-    step_e = []
-    two = pl.ds(SEQ, 2)
-    for o, d in enumerate(peers):
-        step_e.append(remote(tsend.at[d, two], rt.at[me, two], t_s.at[4, o], t_r.at[4, o], {"seq": d}))
-    step_t = []
-    for kk in range(NX):
-        four = pl.ds(kk * 4, 4)
-        for o, d in enumerate(peers):
-            copy = pltpu.make_async_remote_copy(
-                src_ref=tsend.at[d, four], dst_ref=rt.at[me, four], send_sem=t_s.at[kk, o],
-                recv_sem=t_r.at[kk, o], device_id={"seq": d}, device_id_type=MESH,
-            )
-            if kk == 0:
-                copy.start()
-            step_t.append(copy)
+    step_e = [term(4, SEQ, 2, o) for o in range(SEQ - 1)]
+    step_t = [term(kk, kk * 4, 4, o) for kk in range(NX) for o in range(SEQ - 1)]
     rt[me] = tsend[me]
     for copy in step_e:
         copy.wait_recv()
@@ -516,50 +509,60 @@
     )(*operands)
 
 
-def spread_kernel(summed, pair, prefix, down, rise, pair_out, prefix_out):
+def spread_kernel(summed, pair, prefix, down, rise, pair_out, prefix_out, got, made, risen, sem_got, sem_made):
     factor = 2.0 / (GRP * SEQ)
-    step = pl.program_id(0)
-
-    @pl.when(step < 5)
-    def _():
+    arrive = [pltpu.make_async_copy(summed.at[i], got.at[i], sem_got.at[i]) for i in range(2 * TYPES)]
+    leave = [
+        pltpu.make_async_copy(pair, pair_out, sem_made.at[0]),
+        pltpu.make_async_copy(prefix, prefix_out, sem_made.at[1]),
+    ]
+    for copy in arrive + leave:
+        copy.start()
+    for i in range(2 * TYPES):
+        arrive[i].wait()
         for a in range(NX):
-            part = summed[0, a].reshape(BLK, TILE).astype(f32)
-            down[:, a * TILE : (a + 1) * TILE] = part * factor
-
-    @pl.when(step == 0)
-    def _():
-        pair_out[...] = pair[...]
-        prefix_out[...] = prefix[...]
-
-    @pl.when(step == 5)
-    def _():
-        for a in range(NX):
-            part = summed[0, a].reshape(BLK, TILE).astype(f32)
-            side = a // 2
-            rise[side, :, (a % 2) * TILE : (a % 2 + 1) * TILE] = part[side * 64 : side * 64 + 64] * factor
+            part = got[i, a].reshape(BLK, TILE).astype(f32) * factor
+            if i < 5:
+                made[i, :, a * TILE : (a + 1) * TILE] = part
+            else:
+                side = a // 2
+                risen[side, :, (a % 2) * TILE : (a % 2 + 1) * TILE] = part[side * 64 : side * 64 + 64]
+        if i < 5:
+            for half in range(2):
+                cut = slice(half * 64, half * 64 + 64)
+                leave.append(
+                    pltpu.make_async_copy(
+                        made.at[i, cut], down.at[cut, i * NX * TILE : (i + 1) * NX * TILE],
+                        sem_made.at[2 + 2 * i + half],
+                    )
+                )
+                leave[-1].start()
+        else:
+            leave.append(pltpu.make_async_copy(risen, rise, sem_made.at[12]))
+            leave[-1].start()
+    for copy in leave:
+        copy.wait()
 
 
 def spread(summed, pair, prefix):
     return pl.pallas_call(
         spread_kernel,
-        grid=(2 * TYPES,),
         out_shape=(
             jax.ShapeDtypeStruct((BLK, D), f32),
             jax.ShapeDtypeStruct((2, 64, KVW), f32),
             jax.ShapeDtypeStruct((BLK, 2 * KVW), bf16),
             jax.ShapeDtypeStruct((SPAN, 2 * KVW), f32),
         ),
-        in_specs=[
-            pl.BlockSpec((1, NX, SEQ, SPAN, TILE), lambda b: (b, 0, 0, 0, 0)),
-            pl.BlockSpec((BLK, 2 * KVW), lambda b: (0, 0)),
-            pl.BlockSpec((SPAN, 2 * KVW), lambda b: (0, 0)),
+        in_specs=[hbm()] * 3,
+        out_specs=(hbm(),) * 4,
+        scratch_shapes=[
+            pltpu.VMEM((2 * TYPES, NX, SEQ, SPAN, TILE), bf16),
+            pltpu.VMEM((5, BLK, NX * TILE), f32),
+            pltpu.VMEM((2, 64, KVW), f32),
+            pltpu.SemaphoreType.DMA((2 * TYPES,)),
+            pltpu.SemaphoreType.DMA((13,)),
         ],
-        out_specs=(
-            pl.BlockSpec((BLK, NX * TILE), lambda b: (0, jnp.minimum(b, 4))),
-            pl.BlockSpec((2, 64, KVW), lambda b: (0, 0, 0)),
-            pl.BlockSpec((BLK, 2 * KVW), lambda b: (0, 0)),
-            pl.BlockSpec((SPAN, 2 * KVW), lambda b: (0, 0)),
-        ),
+        compiler_params=pltpu.CompilerParams(vmem_limit_bytes=60 * 2**20),
         name="spread",
     )(summed.reshape(2 * TYPES, NX, SEQ, SPAN, TILE), pair, prefix)
 

time: 92.2 us -> 95.3 us (1.034)
  Pallas kernels: 91.3 us -> 94.5 us
    pallas_call x1, Pallas kernels: 5.09 us -> 10.2 us  [spread(): pl.pallas_call(spread_kernel, out_shape=(jax.ShapeDtypeStruct((BLK, D), f...]
    pallas_call x1, Pallas kernels: 86.2 us -> 84.3 us  [backward(): pl.pallas_call(kernel, out_shape=(jax.ShapeDtypeStruct((BLK, 2 * KVW), bf...]
where the time goes in v5:
time: 95.3 us; the launch traced here: 95.1 us
  Pallas kernels  94.5 us (99%)
    pallas_call x1, Pallas kernels, backward(): pl.pallas_call(kernel, out_shape=(jax.ShapeDtypeStruct((BLK, 2 * KVW), bf...  84.3 us
    pallas_call x1, Pallas kernels, spread(): pl.pallas_call(spread_kernel, out_shape=(jax.ShapeDtypeStruct((BLK, D), f...  10.2 us

profile of v5, /device:TPU:1, one launch (start us, length us, event | category | flops | bytes accessed | tf_op | source)
XLA Modules:
  0.0 95.1 jit_solution(3165508213276727807)
XLA Ops:
  0.6 84.3 %backward.1 = (bf16[128,1024]{1,0:T(8,128)(2,1)}, f32[8,1024]{1,0:T(8,128)}, bf16[2,3,4,16,8,256]{5,4,3,2,1,0:T(8,128)(2,1)}) custom-call(s32[16,16]{1,0:T(8,128)} %bitcast.26, s32[1,2]{1,0:T(1,128)} %listed.1, bf16[128,2560]{1,0:T(8,128)(2,1)} %bitcast.18, bf16[128,2560]{1,0:T(8,128)(2,1)} %bitcast.19, bf16[128,2560]{1,0:T(8,128)(2,1)} %bitcast.20, ...), custom_call_target="tpu_custom_call" | custom-call | tf_op jit(solution)/shard_map/backward/pallas_call | solution.py:474
  84.9 10.2 %spread.1 = (f32[128,5120]{1,0:T(8,128)}, f32[2,64,512]{2,1,0:T(8,128)}, bf16[128,1024]{1,0:T(8,128)(2,1)}, f32[8,1024]{1,0:T(8,128)}) custom-call(bf16[6,4,16,8,256]{4,3,2,1,0:T(8,128)(2,1)} %bitcast.16, bf16[128,1024]{1,0:T(8,128)(2,1)} %get-tuple-element.12.pair, f32[8,1024]{1,0:T(8,128)} %get-tuple-element.13.prefix), custom_call_target="tpu_custom_call" | custom-call | tf_op jit(solution)/shard_map/spread/pallas_call | solution.py:548

commit v6 on v5

--- a/solution.py
+++ b/solution.py
@@ -342,6 +342,37 @@
     step_e = [term(4, SEQ, 2, o) for o in range(SEQ - 1)]
     step_t = [term(kk, kk * 4, 4, o) for kk in range(NX) for o in range(SEQ - 1)]
     rt[me] = tsend[me]
+    step_b = [
+        pltpu.make_async_remote_copy(
+            src_ref=back_s.at[peers[o]], dst_ref=back_r.at[me], send_sem=b_s.at[o], recv_sem=b_r.at[o],
+            device_id={"seq": peers[o]}, device_id_type=MESH,
+        )
+        for o in range(SEQ - 1)
+    ]
+
+    def finish(m):
+        for copy in step_t[m * 15 : m * 15 + 15]:
+            copy.wait_recv()
+        span = slice(m * 32, m * 32 + 32)
+        for h in range(KV):
+            for side in range(2):
+                lanes = slice(side * HEAD, (side + 1) * HEAD)
+                place = slice(side * KVW + h * HEAD, side * KVW + (h + 1) * HEAD)
+                total = rt[NX * h, 4 * m : 4 * m + 4, :, lanes].astype(f32)
+                for a in range(1, NX):
+                    total += rt[NX * h + a, 4 * m : 4 * m + 4, :, lanes].astype(f32)
+                all_g[span, place] = total.reshape(32, HEAD).astype(bf16)
+        back = lax.dot_general(all_g[span, :], up[...], NT, preferred_element_type=f32)
+        back_s[4 * m : 4 * m + 4] = back.reshape(4, SPAN, HEAD).astype(bf16)
+        for j in range(4 * m, 4 * m + 4):
+
+            @pl.when(me != j)
+            def _():
+                o = lax.rem(j - me + 2 * SEQ - 1, SEQ)
+                remote(back_s.at[j], back_r.at[me], b_s.at[o], b_r.at[o], {"seq": j})
+
+    for m in (3, 2, 1):
+        finish(m)
     for copy in step_e:
         copy.wait_recv()
     for h in range(KV):
@@ -359,21 +390,7 @@
     for i in range(1, GRP):
         b = lax.rem(grp + i, GRP)
         step_p.append(remote(pt.at[b], rp.at[1 + i], p_s.at[i], p_r.at[i], {"grp": b}))
-    for copy in step_t:
-        copy.wait_recv()
-    for h in range(KV):
-        for side in range(2):
-            lanes = slice(side * HEAD, (side + 1) * HEAD)
-            place = slice(side * KVW + h * HEAD, side * KVW + (h + 1) * HEAD)
-            total = rt[NX * h, 0:SEQ, :, lanes].astype(f32)
-            for a in range(1, NX):
-                total += rt[NX * h + a, 0:SEQ, :, lanes].astype(f32)
-            all_g[0:BLK, place] = total.reshape(BLK, HEAD).astype(bf16)
-    back = lax.dot_general(all_g[0:BLK, :], up[...], NT, preferred_element_type=f32)
-    back_s[...] = back.reshape(SEQ, SPAN, HEAD).astype(bf16)
-    step_b = []
-    for o, d in enumerate(peers):
-        step_b.append(remote(back_s.at[d], back_r.at[me], b_s.at[o], b_r.at[o], {"seq": d}))
+    finish(0)
     back_r[me] = back_s[me]
     for copy in step_p:
         copy.wait_recv()
@@ -509,15 +526,16 @@
     )(*operands)
 
 
-def spread_kernel(summed, pair, prefix, down, rise, pair_out, prefix_out, got, made, risen, sem_got, sem_made):
+def spread_kernel(summed, pair, prefix, down, rise, pair_out, prefix_out, got, made, risen, pair_got, prefix_got, sem_got, sem_made):
     factor = 2.0 / (GRP * SEQ)
     arrive = [pltpu.make_async_copy(summed.at[i], got.at[i], sem_got.at[i]) for i in range(2 * TYPES)]
-    leave = [
-        pltpu.make_async_copy(pair, pair_out, sem_made.at[0]),
-        pltpu.make_async_copy(prefix, prefix_out, sem_made.at[1]),
+    through = [
+        pltpu.make_async_copy(pair, pair_got, sem_got.at[6]),
+        pltpu.make_async_copy(prefix, prefix_got, sem_got.at[7]),
     ]
-    for copy in arrive + leave:
+    for copy in arrive + through:
         copy.start()
+    leave = []
     for i in range(2 * TYPES):
         arrive[i].wait()
         for a in range(NX):
@@ -540,6 +558,10 @@
         else:
             leave.append(pltpu.make_async_copy(risen, rise, sem_made.at[12]))
             leave[-1].start()
+    for i, (source, target) in enumerate(((pair_got, pair_out), (prefix_got, prefix_out))):
+        through[i].wait()
+        leave.append(pltpu.make_async_copy(source, target, sem_made.at[i]))
+        leave[-1].start()
     for copy in leave:
         copy.wait()
 
@@ -559,7 +581,9 @@
             pltpu.VMEM((2 * TYPES, NX, SEQ, SPAN, TILE), bf16),
             pltpu.VMEM((5, BLK, NX * TILE), f32),
             pltpu.VMEM((2, 64, KVW), f32),
-            pltpu.SemaphoreType.DMA((2 * TYPES,)),
+            pltpu.VMEM((BLK, 2 * KVW), bf16),
+            pltpu.VMEM((SPAN, 2 * KVW), f32),
+            pltpu.SemaphoreType.DMA((2 * TYPES + 2,)),
             pltpu.SemaphoreType.DMA((13,)),
         ],
         compiler_params=pltpu.CompilerParams(vmem_limit_bytes=60 * 2**20),

time: 95.3 us -> 87.8 us (0.921)
  Pallas kernels: 94.5 us -> 87 us
    pallas_call x1, Pallas kernels: 10.2 us -> 2.82 us  [spread(): pl.pallas_call(spread_kernel, out_shape=(jax.ShapeDtypeStruct((BLK, D), f...]
where the time goes in v6:
time: 87.8 us; the launch traced here: 87.6 us
  Pallas kernels  87 us (99%)
    pallas_call x1, Pallas kernels, backward(): pl.pallas_call(kernel, out_shape=(jax.ShapeDtypeStruct((BLK, 2 * KVW), bf...  84.2 us
    pallas_call x1, Pallas kernels, spread(): pl.pallas_call(spread_kernel, out_shape=(jax.ShapeDtypeStruct((BLK, D), f...  2.82 us

profile of v6, /device:TPU:1, one launch (start us, length us, event | category | flops | bytes accessed | tf_op | source)
XLA Modules:
  0.0 87.6 jit_solution(10141766983637176880)
XLA Ops:
  0.6 84.2 %backward.1 = (bf16[128,1024]{1,0:T(8,128)(2,1)}, f32[8,1024]{1,0:T(8,128)}, bf16[2,3,4,16,8,256]{5,4,3,2,1,0:T(8,128)(2,1)}) custom-call(s32[16,16]{1,0:T(8,128)} %bitcast.26, s32[1,2]{1,0:T(1,128)} %listed.1, bf16[128,2560]{1,0:T(8,128)(2,1)} %bitcast.18, bf16[128,2560]{1,0:T(8,128)(2,1)} %bitcast.19, bf16[128,2560]{1,0:T(8,128)(2,1)} %bitcast.20, ...), custom_call_target="tpu_custom_call" | custom-call | tf_op jit(solution)/shard_map/backward/pallas_call | solution.py:491
  84.8 2.8 %spread.1 = (f32[128,5120]{1,0:T(8,128)}, f32[2,64,512]{2,1,0:T(8,128)}, bf16[128,1024]{1,0:T(8,128)(2,1)}, f32[8,1024]{1,0:T(8,128)}) custom-call(bf16[6,4,16,8,256]{4,3,2,1,0:T(8,128)(2,1)} %bitcast.16, bf16[128,1024]{1,0:T(8,128)(2,1)} %get-tuple-element.12.pair, f32[8,1024]{1,0:T(8,128)} %get-tuple-element.13.prefix), custom_call_target="tpu_custom_call" | custom-call | tf_op jit(solution)/shard_map/spread/pallas_call | solution.py:570

commit v7 on v6

--- a/solution.py
+++ b/solution.py
@@ -316,17 +316,6 @@
             grads(rows(m, GROUP), score_place(start, m), hides(m), 4)
             return cc
 
-        grads(ends, ends_place(start), [0.0, 0.0], 2)
-
-        @pl.when(step == NX - 1)
-        def _():
-            for i in range(2):
-                part = acc[TREE + i * BLK : TREE + (i + 1) * BLK, :].reshape(SEQ, SPAN, PAIR)
-                tsend[:, SEQ + i, :, 0:HEAD] = (part[:, :, 0:HEAD] * SCALE).astype(bf16)
-                tsend[:, SEQ + i, :, HEAD:PAIR] = part[:, :, HEAD:PAIR].astype(bf16)
-            for o in range(SEQ - 1):
-                term(4, SEQ, 2, o).start()
-
         grads_group(kk, 0)
         for b in range(4):
             j = kk * 4 + b
@@ -336,6 +325,17 @@
         for o in range(SEQ - 1):
             term(kk, kk * 4, 4, o).start()
         lax.fori_loop(0, kk, grads_group, 0)
+        grads(ends, ends_place(start), [0.0, 0.0], 2)
+
+        @pl.when(step == NX - 1)
+        def _():
+            for i in range(2):
+                part = acc[TREE + i * BLK : TREE + (i + 1) * BLK, :].reshape(SEQ, SPAN, PAIR)
+                tsend[:, SEQ + i, :, 0:HEAD] = (part[:, :, 0:HEAD] * SCALE).astype(bf16)
+                tsend[:, SEQ + i, :, HEAD:PAIR] = part[:, :, HEAD:PAIR].astype(bf16)
+            for o in range(SEQ - 1):
+                term(4, SEQ, 2, o).start()
+
         return carry
 
     lax.fori_loop(0, NX, rollout, 0)
@@ -371,8 +371,9 @@
                 o = lax.rem(j - me + 2 * SEQ - 1, SEQ)
                 remote(back_s.at[j], back_r.at[me], b_s.at[o], b_r.at[o], {"seq": j})
 
-    for m in (3, 2, 1):
+    for m in (3, 2, 1, 0):
         finish(m)
+    back_r[me] = back_s[me]
     for copy in step_e:
         copy.wait_recv()
     for h in range(KV):
@@ -390,8 +391,6 @@
     for i in range(1, GRP):
         b = lax.rem(grp + i, GRP)
         step_p.append(remote(pt.at[b], rp.at[1 + i], p_s.at[i], p_r.at[i], {"grp": b}))
-    finish(0)
-    back_r[me] = back_s[me]
     for copy in step_p:
         copy.wait_recv()
     total = pt[grp]
@@ -419,15 +418,20 @@
     back_t[...] = lax.dot_general(eye, back_all[...], NT, preferred_element_type=f32).astype(bf16)
     sibling = {"grp": grp + 1 - 2 * c}
     zero, first, second, third, fourth, fifth = [], [], [], [], [], []
+
+    def down_terms(half, t):
+        for a in range(NX):
+            cut = cols((half * TYPES + t) * NX + a, TILE)
+            s0[half, t, a] = jnp.dot(back_t[...], own_h[:, cut], preferred_element_type=f32).astype(bf16)
+
     for t in range(TYPES):
-        for half in range(2):
-            for a in range(NX):
-                n = (half * TYPES + t) * NX + a
-                if n < D // TILE:
-                    cut = slice(n * TILE, (n + 1) * TILE)
-                    part = jnp.dot(back_t[...], own_h[:, cut], preferred_element_type=f32)
-                    s0[half, t, a] = part.astype(bf16)
+        if t < 2:
+            down_terms(1 - c, t)
+        else:
+            down_terms(0, t)
         zero.append(remote(s0.at[1 - c, t], r0.at[t], s0_s.at[t], s0_r.at[t], sibling))
+    for t in range(2):
+        down_terms(c, t)
     for t in range(TYPES):
         zero[t].wait_recv()
         for a in range(NX):

time: 87.8 us -> 88.4 us (level)
  no operation moved by 1% of the time
where the time goes in v7:
time: 88.4 us; the launch traced here: 88.3 us
  Pallas kernels  87.6 us (99%)
    pallas_call x1, Pallas kernels, backward(): pl.pallas_call(kernel, out_shape=(jax.ShapeDtypeStruct((BLK, 2 * KVW), bf...  84.8 us
    pallas_call x1, Pallas kernels, spread(): pl.pallas_call(spread_kernel, out_shape=(jax.ShapeDtypeStruct((BLK, D), f...  2.82 us

profile of v7, /device:TPU:1, one launch (start us, length us, event | category | flops | bytes accessed | tf_op | source)
XLA Modules:
  0.0 88.3 jit_solution(17614290520345793648)
XLA Ops:
  0.6 84.8 %backward.1 = (bf16[128,1024]{1,0:T(8,128)(2,1)}, f32[8,1024]{1,0:T(8,128)}, bf16[2,3,4,16,8,256]{5,4,3,2,1,0:T(8,128)(2,1)}) custom-call(s32[16,16]{1,0:T(8,128)} %bitcast.26, s32[1,2]{1,0:T(1,128)} %listed.1, bf16[128,2560]{1,0:T(8,128)(2,1)} %bitcast.18, bf16[128,2560]{1,0:T(8,128)(2,1)} %bitcast.19, bf16[128,2560]{1,0:T(8,128)(2,1)} %bitcast.20, ...), custom_call_target="tpu_custom_call" | custom-call | tf_op jit(solution)/shard_map/backward/pallas_call | solution.py:495
  85.4 2.8 %spread.1 = (f32[128,5120]{1,0:T(8,128)}, f32[2,64,512]{2,1,0:T(8,128)}, bf16[128,1024]{1,0:T(8,128)(2,1)}, f32[8,1024]{1,0:T(8,128)}) custom-call(bf16[6,4,16,8,256]{4,3,2,1,0:T(8,128)(2,1)} %bitcast.16, bf16[128,1024]{1,0:T(8,128)(2,1)} %get-tuple-element.12.pair, f32[8,1024]{1,0:T(8,128)} %get-tuple-element.13.prefix), custom_call_target="tpu_custom_call" | custom-call | tf_op jit(solution)/shard_map/spread/pallas_call | solution.py:574

commit v8 on v6

--- a/solution.py
+++ b/solution.py
@@ -77,7 +77,7 @@
     pair, prefix, out,
     q_in, g_in, delta_in, kv, own_g, own_s, own_h, own_p, down, pool, up, delta_out, all_g, back_all, back_t, proj_all, proj_t,
     s_ref, acc, qs, gs, pb, dsb, stat, diag,
-    tsend, rt, proj_s, proj_r, pt, rp, back_s, back_r,
+    tsend, rt, proj_s, proj_r, pt, rp, rq, back_s, back_r,
     s0, r0, s1, r1, s2, r2, full, own_x,
     sem_in, kvx_s, kvx_r, kvy_s, kvy_r, q_s, q_r, t_s, t_r, j_s, j_r, b_s, b_r, p_s, p_r,
     s0_s, s0_r, s1_s, s1_r, s2_s, s2_r, a2_s, a2_r, a1_s, a1_r, a0_s, a0_r,
@@ -385,18 +385,19 @@
                     part += rt[NX * h + a, SEQ + i, :, lanes].astype(f32)
                 rp[i, :, place] = part
     for b in range(GRP):
-        pt[b] = rp[0] * (listed[0, 0] == b).astype(f32) + rp[1] * (listed[0, 1] == b).astype(f32)
+        part = rp[0] * (listed[0, 0] == b).astype(f32) + rp[1] * (listed[0, 1] == b).astype(f32)
+        pt[b] = part.astype(bf16)
     step_p = []
     for i in range(1, GRP):
         b = lax.rem(grp + i, GRP)
-        step_p.append(remote(pt.at[b], rp.at[1 + i], p_s.at[i], p_r.at[i], {"grp": b}))
+        step_p.append(remote(pt.at[b], rq.at[i], p_s.at[i], p_r.at[i], {"grp": b}))
     finish(0)
     back_r[me] = back_s[me]
     for copy in step_p:
         copy.wait_recv()
-    total = pt[grp]
+    total = pt[grp].astype(f32)
     for i in range(1, GRP):
-        total += rp[1 + i]
+        total += rq[i].astype(f32)
     own_x[...] = total
     keep.append(local(own_x, prefix, 12))
     tail = jnp.concatenate([total, jnp.zeros_like(total)], axis=0).astype(bf16)
@@ -419,15 +420,20 @@
     back_t[...] = lax.dot_general(eye, back_all[...], NT, preferred_element_type=f32).astype(bf16)
     sibling = {"grp": grp + 1 - 2 * c}
     zero, first, second, third, fourth, fifth = [], [], [], [], [], []
+
+    def down_terms(half, t):
+        for a in range(NX):
+            cut = cols((half * TYPES + t) * NX + a, TILE)
+            s0[half, t, a] = jnp.dot(back_t[...], own_h[:, cut], preferred_element_type=f32).astype(bf16)
+
     for t in range(TYPES):
-        for half in range(2):
-            for a in range(NX):
-                n = (half * TYPES + t) * NX + a
-                if n < D // TILE:
-                    cut = slice(n * TILE, (n + 1) * TILE)
-                    part = jnp.dot(back_t[...], own_h[:, cut], preferred_element_type=f32)
-                    s0[half, t, a] = part.astype(bf16)
+        if t < 2:
+            down_terms(1 - c, t)
+        else:
+            down_terms(0, t)
         zero.append(remote(s0.at[1 - c, t], r0.at[t], s0_s.at[t], s0_r.at[t], sibling))
+    for t in range(2):
+        down_terms(c, t)
     for t in range(TYPES):
         zero[t].wait_recv()
         for a in range(NX):
@@ -506,7 +512,7 @@
             low(GROUP, W), low(GROUP, W), wide(2, NX, 8, W), wide(GROUP, BLK),
             low(SEQ, SEQ + 2, SPAN, PAIR), low(SEQ, SEQ + 2, SPAN, PAIR),
             low(SEQ, SPAN, HEAD), low(SEQ, SPAN, HEAD),
-            wide(GRP, SPAN, 2 * KVW), wide(GRP + 1, SPAN, 2 * KVW),
+            low(GRP, SPAN, 2 * KVW), wide(2, SPAN, 2 * KVW), low(GRP, SPAN, 2 * KVW),
             low(SEQ, SPAN, HEAD), low(SEQ, SPAN, HEAD),
             low(2, TYPES, NX, BLK, TILE), low(TYPES, NX, BLK, TILE), low(TYPES, NX, BLK, TILE),
             low(TYPES, NX - 1, BLK, TILE), low(TYPES, SEQ, SPAN, TILE), low(TYPES, SEQ - 1, SPAN, TILE),

time: 87.8 us -> 87.9 us (level)
  no operation moved by 1% of the time
where the time goes in v8:
time: 87.9 us; the launch traced here: 87.8 us
  Pallas kernels  87.1 us (99%)
    pallas_call x1, Pallas kernels, backward(): pl.pallas_call(kernel, out_shape=(jax.ShapeDtypeStruct((BLK, 2 * KVW), bf...  84.3 us
    pallas_call x1, Pallas kernels, spread(): pl.pallas_call(spread_kernel, out_shape=(jax.ShapeDtypeStruct((BLK, D), f...  2.82 us

profile of v8, /device:TPU:1, one launch (start us, length us, event | category | flops | bytes accessed | tf_op | source)
XLA Modules:
  0.0 87.8 jit_solution(2978480350849038223)
XLA Ops:
  0.6 84.3 %backward.1 = (bf16[128,1024]{1,0:T(8,128)(2,1)}, f32[8,1024]{1,0:T(8,128)}, bf16[2,3,4,16,8,256]{5,4,3,2,1,0:T(8,128)(2,1)}) custom-call(s32[16,16]{1,0:T(8,128)} %bitcast.26, s32[1,2]{1,0:T(1,128)} %listed.1, bf16[128,2560]{1,0:T(8,128)(2,1)} %bitcast.18, bf16[128,2560]{1,0:T(8,128)(2,1)} %bitcast.19, bf16[128,2560]{1,0:T(8,128)(2,1)} %bitcast.20, ...), custom_call_target="tpu_custom_call" | custom-call | tf_op jit(solution)/shard_map/backward/pallas_call | solution.py:497
  84.9 2.8 %spread.1 = (f32[128,5120]{1,0:T(8,128)}, f32[2,64,512]{2,1,0:T(8,128)}, bf16[128,1024]{1,0:T(8,128)(2,1)}, f32[8,1024]{1,0:T(8,128)}) custom-call(bf16[6,4,16,8,256]{4,3,2,1,0:T(8,128)(2,1)} %bitcast.16, bf16[128,1024]{1,0:T(8,128)(2,1)} %get-tuple-element.12.pair, f32[8,1024]{1,0:T(8,128)} %get-tuple-element.13.prefix), custom_call_target="tpu_custom_call" | custom-call | tf_op jit(solution)/shard_map/spread/pallas_call | solution.py:576

commit v9 on v6

--- a/solution.py
+++ b/solution.py
@@ -212,7 +212,7 @@
     query_at = lax.broadcasted_iota(jnp.int32, (GROUP, BLK), 1)
     diag[...] = jnp.where(key_at <= y * BLK + query_at, 0.0, MASKED).astype(f32)
     keep[2].wait()
-    for copy in step_q + step_y[0]:
+    for copy in step_y[0]:
         copy.wait_recv()
 
     def score_rows(kk):
@@ -227,7 +227,16 @@
     ends = slice(TREE, TREE + 2 * BLK)
 
     def scores(step, carry):
-        kk = NX - 1 - step
+        off = step + step // 2 * (1 - 2 * lax.rem(step, 2))
+        kk = lax.rem(x + NX - off, NX)
+
+        @pl.when(step > 0)
+        def _():
+            pltpu.make_async_remote_copy(
+                src_ref=q.at[:, 0:DT], dst_ref=q_in.at[kk], send_sem=q_s.at[0, off], recv_sem=q_r.at[0, off],
+                device_id={"seq": lax.rem(x + off, NX) * NX + y}, device_id_type=MESH,
+            ).wait_recv()
+
         r = y + NX * kk
         start = score_rows(kk)
         for t in range(REP):

time: 87.8 us -> 87.9 us (level)
  no operation moved by 1% of the time
where the time goes in v9:
time: 87.9 us; the launch traced here: 87.7 us
  Pallas kernels  87 us (99%)
    pallas_call x1, Pallas kernels, backward(): pl.pallas_call(kernel, out_shape=(jax.ShapeDtypeStruct((BLK, 2 * KVW), bf...  84.2 us
    pallas_call x1, Pallas kernels, spread(): pl.pallas_call(spread_kernel, out_shape=(jax.ShapeDtypeStruct((BLK, D), f...  2.82 us

profile of v9, /device:TPU:1, one launch (start us, length us, event | category | flops | bytes accessed | tf_op | source)
XLA Modules:
  0.0 87.7 jit_solution(15707668988224610922)
XLA Ops:
  0.6 84.2 %backward.1 = (bf16[128,1024]{1,0:T(8,128)(2,1)}, f32[8,1024]{1,0:T(8,128)}, bf16[2,3,4,16,8,256]{5,4,3,2,1,0:T(8,128)(2,1)}) custom-call(s32[16,16]{1,0:T(8,128)} %bitcast.26, s32[1,2]{1,0:T(1,128)} %listed.1, bf16[128,2560]{1,0:T(8,128)(2,1)} %bitcast.18, bf16[128,2560]{1,0:T(8,128)(2,1)} %bitcast.19, bf16[128,2560]{1,0:T(8,128)(2,1)} %bitcast.20, ...), custom_call_target="tpu_custom_call" | custom-call | tf_op jit(solution)/shard_map/backward/pallas_call | solution.py:500
  84.8 2.8 %spread.1 = (f32[128,5120]{1,0:T(8,128)}, f32[2,64,512]{2,1,0:T(8,128)}, bf16[128,1024]{1,0:T(8,128)(2,1)}, f32[8,1024]{1,0:T(8,128)}) custom-call(bf16[6,4,16,8,256]{4,3,2,1,0:T(8,128)(2,1)} %bitcast.16, bf16[128,1024]{1,0:T(8,128)(2,1)} %get-tuple-element.12.pair, f32[8,1024]{1,0:T(8,128)} %get-tuple-element.13.prefix), custom_call_target="tpu_custom_call" | custom-call | tf_op jit(solution)/shard_map/spread/pallas_call | solution.py:579

commit v10 on v7

--- a/solution.py
+++ b/solution.py
@@ -77,7 +77,7 @@
     pair, prefix, out,
     q_in, g_in, delta_in, kv, own_g, own_s, own_h, own_p, down, pool, up, delta_out, all_g, back_all, back_t, proj_all, proj_t,
     s_ref, acc, qs, gs, pb, dsb, stat, diag,
-    tsend, rt, proj_s, proj_r, pt, rp, back_s, back_r,
+    tsend, rt, proj_s, proj_r, pt, rp, rq, back_s, back_r,
     s0, r0, s1, r1, s2, r2, full, own_x,
     sem_in, kvx_s, kvx_r, kvy_s, kvy_r, q_s, q_r, t_s, t_r, j_s, j_r, b_s, b_r, p_s, p_r,
     s0_s, s0_r, s1_s, s1_r, s2_s, s2_r, a2_s, a2_r, a1_s, a1_r, a0_s, a0_r,
@@ -212,7 +212,7 @@
     query_at = lax.broadcasted_iota(jnp.int32, (GROUP, BLK), 1)
     diag[...] = jnp.where(key_at <= y * BLK + query_at, 0.0, MASKED).astype(f32)
     keep[2].wait()
-    for copy in step_q + step_y[0]:
+    for copy in step_y[0]:
         copy.wait_recv()
 
     def score_rows(kk):
@@ -227,7 +227,16 @@
     ends = slice(TREE, TREE + 2 * BLK)
 
     def scores(step, carry):
-        kk = NX - 1 - step
+        off = step + step // 2 * (1 - 2 * lax.rem(step, 2))
+        kk = lax.rem(x + NX - off, NX)
+
+        @pl.when(step > 0)
+        def _():
+            pltpu.make_async_remote_copy(
+                src_ref=q.at[:, 0:DT], dst_ref=q_in.at[kk], send_sem=q_s.at[0, off], recv_sem=q_r.at[0, off],
+                device_id={"seq": lax.rem(x + off, NX) * NX + y}, device_id_type=MESH,
+            ).wait_recv()
+
         r = y + NX * kk
         start = score_rows(kk)
         for t in range(REP):
@@ -386,16 +395,17 @@
                     part += rt[NX * h + a, SEQ + i, :, lanes].astype(f32)
                 rp[i, :, place] = part
     for b in range(GRP):
-        pt[b] = rp[0] * (listed[0, 0] == b).astype(f32) + rp[1] * (listed[0, 1] == b).astype(f32)
+        part = rp[0] * (listed[0, 0] == b).astype(f32) + rp[1] * (listed[0, 1] == b).astype(f32)
+        pt[b] = part.astype(bf16)
     step_p = []
     for i in range(1, GRP):
         b = lax.rem(grp + i, GRP)
-        step_p.append(remote(pt.at[b], rp.at[1 + i], p_s.at[i], p_r.at[i], {"grp": b}))
+        step_p.append(remote(pt.at[b], rq.at[i], p_s.at[i], p_r.at[i], {"grp": b}))
     for copy in step_p:
         copy.wait_recv()
-    total = pt[grp]
+    total = pt[grp].astype(f32)
     for i in range(1, GRP):
-        total += rp[1 + i]
+        total += rq[i].astype(f32)
     own_x[...] = total
     keep.append(local(own_x, prefix, 12))
     tail = jnp.concatenate([total, jnp.zeros_like(total)], axis=0).astype(bf16)
@@ -510,7 +520,7 @@
             low(GROUP, W), low(GROUP, W), wide(2, NX, 8, W), wide(GROUP, BLK),
             low(SEQ, SEQ + 2, SPAN, PAIR), low(SEQ, SEQ + 2, SPAN, PAIR),
             low(SEQ, SPAN, HEAD), low(SEQ, SPAN, HEAD),
-            wide(GRP, SPAN, 2 * KVW), wide(GRP + 1, SPAN, 2 * KVW),
+            low(GRP, SPAN, 2 * KVW), wide(2, SPAN, 2 * KVW), low(GRP, SPAN, 2 * KVW),
             low(SEQ, SPAN, HEAD), low(SEQ, SPAN, HEAD),
             low(2, TYPES, NX, BLK, TILE), low(TYPES, NX, BLK, TILE), low(TYPES, NX, BLK, TILE),
             low(TYPES, NX - 1, BLK, TILE), low(TYPES, SEQ, SPAN, TILE), low(TYPES, SEQ - 1, SPAN, TILE),

time: 88.4 us -> 87.6 us (level)
  no operation moved by 1% of the time
where the time goes in v10:
time: 87.6 us; the launch traced here: 87.4 us
  Pallas kernels  86.8 us (99%)
    pallas_call x1, Pallas kernels, backward(): pl.pallas_call(kernel, out_shape=(jax.ShapeDtypeStruct((BLK, 2 * KVW), bf...  84 us
    pallas_call x1, Pallas kernels, spread(): pl.pallas_call(spread_kernel, out_shape=(jax.ShapeDtypeStruct((BLK, D), f...  2.82 us

profile of v10, /device:TPU:1, one launch (start us, length us, event | category | flops | bytes accessed | tf_op | source)
XLA Modules:
  0.0 87.4 jit_solution(2031826750001689912)
XLA Ops:
  0.6 84.0 %backward.1 = (bf16[128,1024]{1,0:T(8,128)(2,1)}, f32[8,1024]{1,0:T(8,128)}, bf16[2,3,4,16,8,256]{5,4,3,2,1,0:T(8,128)(2,1)}) custom-call(s32[16,16]{1,0:T(8,128)} %bitcast.26, s32[1,2]{1,0:T(1,128)} %listed.1, bf16[128,2560]{1,0:T(8,128)(2,1)} %bitcast.18, bf16[128,2560]{1,0:T(8,128)(2,1)} %bitcast.19, bf16[128,2560]{1,0:T(8,128)(2,1)} %bitcast.20, ...), custom_call_target="tpu_custom_call" | custom-call | tf_op jit(solution)/shard_map/backward/pallas_call | solution.py:505
  84.6 2.8 %spread.1 = (f32[128,5120]{1,0:T(8,128)}, f32[2,64,512]{2,1,0:T(8,128)}, bf16[128,1024]{1,0:T(8,128)(2,1)}, f32[8,1024]{1,0:T(8,128)}) custom-call(bf16[6,4,16,8,256]{4,3,2,1,0:T(8,128)(2,1)} %bitcast.16, bf16[128,1024]{1,0:T(8,128)(2,1)} %get-tuple-element.12.pair, f32[8,1024]{1,0:T(8,128)} %get-tuple-element.13.prefix), custom_call_target="tpu_custom_call" | custom-call | tf_op jit(solution)/shard_map/spread/pallas_call | solution.py:584
